TPU v7x, 512 devices: a whole 4x4x16 slice. The times are simulated.
512 devices in a mesh: sec: 16 (over z), tile: 32 (over y, x, core).
Axes of the slice: x: 4, y: 4, z: 16, core: 2. Of those that a mesh axis runs over, the one named last changes fastest.
Arguments:
- object_slab: float32 [32, 2, 8192, 256], P('sec', None, 'tile')
- probe: float32 [2, 2, 128, 128], replicated, may hold values from -4 to 4
- amplitudes: bfloat16 [256, 128, 128], P('tile'), may hold values from 0.19921875 to 2
- offsets: int32 [256, 2], P('tile'), may hold values from 0 to 128
- counts: int32 [32], P('tile'), may hold values from 1 to 8, as said below
Outputs:
- object_grad: float32 [32, 2, 8192, 256], P('sec', None, 'tile')
- probe_grad: float32 [65536], P(('sec', 'tile'))
Inputs may be any that keep to these rules, and one draw needn't show every extreme that they name: The first counts[q] slots of tile q are live; some tile has all 8 slots live.
All inputs are finite; a program needn't handle non-finite values.
Results may differ from a plain program's by a relative error of at most 0.04.
Values may be sent and summed in bfloat16 or wider, within the bound.
A program may use at most 64 MiB of HBM per device.

v0:
```python
import math

import jax
import jax.numpy as jnp
from jax import lax
from jax.sharding import PartitionSpec as P

PHASE_SCALE = 20.0


def from_behind(value, axis, steps):
    count = lax.axis_size(axis)
    leading, last = (max(0, -steps), min(count, count - steps))
    return lax.ppermute(value, axis, [(source, source + steps) for source in range(leading, last)])


def matmul_exact(left_matrix, right_matrix):
    return jnp.dot(
        left_matrix,
        right_matrix,
        precision=lax.Precision.HIGHEST,
        preferred_element_type=jnp.float32,
    )


def dft_tables(length):
    indices = lax.iota(jnp.int32, length)
    product = indices[:, None] * indices[None, :] % length
    angles = 2.0 * math.pi / length * product.astype(jnp.float32)
    cosine_table = jnp.cos(angles)
    sine_table = jnp.sin(angles)
    normalize = 1.0 / math.sqrt(length)
    positive = (length - 1) // 2 + 1
    signed = jnp.where(indices < positive, indices, indices - length).astype(jnp.float32) / length
    phases = PHASE_SCALE * signed * signed
    kernel_re = jnp.cos(phases)
    kernel_im = -jnp.sin(phases)
    right_re = kernel_re[:, None] * cosine_table + kernel_im[:, None] * sine_table
    right_im = kernel_im[:, None] * cosine_table - kernel_re[:, None] * sine_table
    prop_re = (matmul_exact(cosine_table, right_re) - matmul_exact(sine_table, right_im)) / length
    prop_im = (matmul_exact(cosine_table, right_im) + matmul_exact(sine_table, right_re)) / length
    return ((cosine_table * normalize, -sine_table * normalize), (prop_re, prop_im))


def left_apply(matrix_in, field_in):
    return jnp.einsum(
        "ac,bmcd->bmad",
        matrix_in,
        field_in,
        precision=lax.Precision.HIGHEST,
        preferred_element_type=jnp.float32,
    )


def right_apply(field_in, matrix_in):
    return jnp.einsum(
        "bmcd,de->bmce",
        field_in,
        matrix_in,
        precision=lax.Precision.HIGHEST,
        preferred_element_type=jnp.float32,
    )


def two_sided(matrix_re, matrix_im, field_in):
    field_re = field_in[:, 0]
    field_im = field_in[:, 1]
    half_re = left_apply(matrix_re, field_re) - left_apply(matrix_im, field_im)
    half_im = left_apply(matrix_re, field_im) + left_apply(matrix_im, field_re)
    out_re = right_apply(half_re, matrix_re) - right_apply(half_im, matrix_im)
    out_im = right_apply(half_re, matrix_im) + right_apply(half_im, matrix_re)
    return jnp.stack([out_re, out_im], axis=1)


def multiply(window, field_in, conj_sign):
    trans_re = window[:, 0][:, None]
    trans_im = conj_sign * window[:, 1][:, None]
    field_re = field_in[:, 0]
    field_im = field_in[:, 1]
    return jnp.stack(
        [trans_re * field_re - trans_im * field_im, trans_re * field_im + trans_im * field_re],
        axis=1,
    )


def far_factor(spectrum, modelled_in, amps_in, live_mask):
    factor = 2.0 * (1.0 - amps_in / modelled_in) * live_mask[:, None, None]
    return spectrum * factor[:, None, None]


def shards(object_slab, probe, amplitudes, offsets, counts):
    length = probe.shape[-1]
    mode_count = probe.shape[0]
    layers = object_slab.shape[0]
    slot_count = offsets.shape[0]
    sections = lax.axis_size("sec")
    section = lax.axis_index("sec")
    (far_re, far_im), (prop_re, prop_im) = dft_tables(length)
    anchor = jnp.zeros((), jnp.int32)

    def cut_window(corner_pair):
        return lax.dynamic_slice(
            object_slab,
            (anchor, anchor, corner_pair[0], corner_pair[1]),
            (layers, 2, length, length),
        )

    per_turn = 2
    blocks = slot_count // per_turn
    wave_shape = (per_turn, 2, mode_count, length, length)
    incident = jnp.broadcast_to(jnp.transpose(probe, (1, 0, 2, 3))[None], wave_shape)

    def windows(first_row):
        chosen = lax.dynamic_slice_in_dim(offsets, first_row, per_turn, 0)
        return (chosen, jax.vmap(cut_window)(chosen))

    def forward_turn(turn_index, loop_state):
        received, stored, exit_waves = loop_state
        block_index = turn_index - section
        active = (block_index >= 0) & (block_index < blocks)
        first_row = jnp.clip(block_index, 0, blocks - 1) * per_turn
        arriving = jnp.where(section == 0, incident, received.astype(jnp.float32))

        def forward_compute_block(operands):
            chosen, patches = windows(first_row)
            field_now = arriving
            entering_list = []
            for stratum in range(layers):
                entering_list.append(field_now)
                field_now = two_sided(
                    prop_re, prop_im, multiply(patches[:, stratum], field_now, 1.0)
                )
            new_stored = lax.dynamic_update_slice_in_dim(
                operands[0], jnp.stack(entering_list, axis=1), first_row, 0
            )
            new_exits = lax.dynamic_update_slice_in_dim(operands[1], field_now, first_row, 0)
            return (new_stored, new_exits, field_now.astype(jnp.bfloat16))

        def forward_skip_block(operands):
            return (operands[0], operands[1], jnp.zeros_like(received))

        stored, exit_waves, outgoing_wave = lax.cond(
            active, forward_compute_block, forward_skip_block, (stored, exit_waves)
        )
        received = from_behind(outgoing_wave, "sec", 1)
        return (received, stored, exit_waves)

    start_state = (
        jnp.zeros(wave_shape, jnp.bfloat16),
        jnp.zeros((slot_count, layers, 2, mode_count, length, length), jnp.float32),
        jnp.zeros((slot_count, 2, mode_count, length, length), jnp.float32),
    )
    ignored, stored, exit_waves = lax.fori_loop(0, blocks + sections - 1, forward_turn, start_state)

    def far_gradient(exit_field):
        spectrum = two_sided(far_re, far_im, exit_field)
        intensity = jnp.sum(spectrum[:, 0] ** 2 + spectrum[:, 1] ** 2, axis=1)
        modelled = jnp.sqrt(intensity + 0.25)
        live_mask = (lax.iota(jnp.int32, slot_count) < counts[0]).astype(jnp.float32)
        return two_sided(
            far_re,
            -far_im,
            far_factor(spectrum, modelled, amplitudes.astype(jnp.float32), live_mask),
        )

    far_seeds = lax.cond(section == sections - 1, far_gradient, jnp.zeros_like, exit_waves)

    def backward_turn(turn_index, loop_state):
        received, slab_grad, probe_total = loop_state
        block_index = turn_index - (sections - 1 - section)
        active = (block_index >= 0) & (block_index < blocks)
        first_row = jnp.clip(block_index, 0, blocks - 1) * per_turn
        local_seed = lax.dynamic_slice_in_dim(far_seeds, first_row, per_turn, 0)
        arriving = jnp.where(section == sections - 1, local_seed, received.astype(jnp.float32))

        def backward_compute_block(operands):
            chosen, patches = windows(first_row)
            entering_now = lax.dynamic_slice_in_dim(stored, first_row, per_turn, 0)
            gradient = arriving
            piece_list = [None] * layers
            for stratum in reversed(range(layers)):
                middle = two_sided(prop_re, -prop_im, gradient)
                before = entering_now[:, stratum]
                piece_re = jnp.sum(
                    before[:, 0] * middle[:, 0] + before[:, 1] * middle[:, 1], axis=1
                )
                piece_im = jnp.sum(
                    before[:, 0] * middle[:, 1] - before[:, 1] * middle[:, 0], axis=1
                )
                piece_list[stratum] = jnp.stack([piece_re, piece_im], axis=1)
                gradient = multiply(patches[:, stratum], middle, -1.0)
            patch_grads = jnp.stack(piece_list, axis=1)
            accumulated = operands[0]
            for member in range(per_turn):
                corner = (anchor, anchor, chosen[member, 0], chosen[member, 1])
                current = lax.dynamic_slice(accumulated, corner, (layers, 2, length, length))
                accumulated = lax.dynamic_update_slice(
                    accumulated, current + patch_grads[member], corner
                )
            return (
                accumulated,
                operands[1] + jnp.sum(gradient, axis=0),
                gradient.astype(jnp.bfloat16),
            )

        def backward_skip_block(operands):
            return (operands[0], operands[1], jnp.zeros_like(received))

        slab_grad, probe_total, outgoing_grad = lax.cond(
            active, backward_compute_block, backward_skip_block, (slab_grad, probe_total)
        )
        received = from_behind(outgoing_grad, "sec", -1)
        return (received, slab_grad, probe_total)

    back_state = (
        jnp.zeros(wave_shape, jnp.bfloat16),
        jnp.zeros(object_slab.shape, jnp.float32),
        jnp.zeros((2, mode_count, length, length), jnp.float32),
    )
    ignored, slab_grad, probe_total = lax.fori_loop(
        0, blocks + sections - 1, backward_turn, back_state
    )
    probe_term = jnp.where(section == 0, probe_total, 0.0)
    flattened = jnp.transpose(probe_term, (1, 0, 2, 3)).reshape(-1)
    probe_grad = lax.psum_scatter(flattened, ("sec", "tile"), scatter_dimension=0, tiled=True)
    return (slab_grad, probe_grad)


def solution(mesh):
    in_specs = (
        P("sec", None, "tile", None),
        P(),
        P("tile", None, None),
        P("tile", None),
        P("tile"),
    )
    out_specs = (P("sec", None, "tile", None), P(("sec", "tile")))
    return jax.shard_map(shards, mesh=mesh, in_specs=in_specs, out_specs=out_specs, check_vma=False)
```

profile of v0, /device:TPU:1, one launch (start us, length us, event | category | flops | bytes accessed | tf_op | source)
XLA Modules:
  0.0 1790.2 jit_solution(16998891625153718921)
XLA Ops:
  13.8 326.4 %while.43 = (s32[]{:T(128)}, bf16[2,2,2,128,128]{4,3,2,0,1:T(8,128)(2,1)S(1)}, f32[8,2,2,2,128,128]{5,4,3,0,2,1:T(8,128)}, f32[8,2,2,128,128]{4,3,2,0,1:T(8,128)...) while((s32[]{:T(128)}, ...), condition=%wide.region_3.4_spmd.clone, body=%wide.region_0.3_spmd.clone.sunk | while | flops 1613889536 | bytes 26477300 | solution.py:153
  14.3 16.1 conditional.8
  34.9 16.0 conditional.8
  58.1 16.0 conditional.8
  81.2 16.0 conditional.8
  104.3 19.7 %collective-permute-start = (bf16[2,2,2,128,128]{4,3,2,0,1:T(8,128)(2,1)S(1)}, bf16[2,2,2,128,128]{4,3,2,0,1:T(8,128)(2,1)S(1)}, u32[]{:S(2)}, u32[]{:S(2)}) collective-permute-start(bf16[2,2,2,128,128]{4,3,2,0,1:T(8,128)(2,1)S(1)} %get-tuple-element.1208), channel_id=1, source_target_pairs={{0,32},{32,64},{64,96},{96,128},{128,160},{160,192},{192,224},{224... | collective-permute-start | bytes 786440 | tf_op jit(solution)/shard_map/while/body/eval_jaxpr/ppermute | solution.py:14
  134.6 17.9 collective-permute-start
  163.0 18.5 %collective-permute-start = (bf16[2,2,2,128,128]{4,3,2,0,1:T(8,128)(2,1)S(1)}, bf16[2,2,2,128,128]{4,3,2,0,1:T(8,128)(2,1)S(1)}, u32[]{:S(2)}, u32[]{:S(2)}) collective-permute-start(bf16[2,2,2,128,128]{4,3,2,0,1:T(8,128)(2,1)S(1)} %get-tuple-element.1208), channel_id=1, source_target_pairs={{0,32},{32,64},{64,96},{96,128},{128,160},{160,192},{192,224},{224... | collective-permute-start | bytes 786440 | tf_op jit(solution)/shard_map/while/body/eval_jaxpr/ppermute | solution.py:14
  184.8 5.1 collective-permute-start
  193.2 20.9 %collective-permute-start = (bf16[2,2,2,128,128]{4,3,2,0,1:T(8,128)(2,1)S(1)}, bf16[2,2,2,128,128]{4,3,2,0,1:T(8,128)(2,1)S(1)}, u32[]{:S(2)}, u32[]{:S(2)}) collective-permute-start(bf16[2,2,2,128,128]{4,3,2,0,1:T(8,128)(2,1)S(1)} %get-tuple-element.1208), channel_id=1, source_target_pairs={{0,32},{32,64},{64,96},{96,128},{128,160},{160,192},{192,224},{224... | collective-permute-start | bytes 786440 | tf_op jit(solution)/shard_map/while/body/eval_jaxpr/ppermute | solution.py:14
  217.5 5.0 collective-permute-start
  225.9 16.6 collective-permute-start
  246.6 4.2 collective-permute-start
  254.2 19.1 %collective-permute-start = (bf16[2,2,2,128,128]{4,3,2,0,1:T(8,128)(2,1)S(1)}, bf16[2,2,2,128,128]{4,3,2,0,1:T(8,128)(2,1)S(1)}, u32[]{:S(2)}, u32[]{:S(2)}) collective-permute-start(bf16[2,2,2,128,128]{4,3,2,0,1:T(8,128)(2,1)S(1)} %get-tuple-element.1208), channel_id=1, source_target_pairs={{0,32},{32,64},{64,96},{96,128},{128,160},{160,192},{192,224},{224... | collective-permute-start | bytes 786440 | tf_op jit(solution)/shard_map/while/body/eval_jaxpr/ppermute | solution.py:14
  273.3 5.7 collective-permute-done
  286.3 19.4 %collective-permute-start = (bf16[2,2,2,128,128]{4,3,2,0,1:T(8,128)(2,1)S(1)}, bf16[2,2,2,128,128]{4,3,2,0,1:T(8,128)(2,1)S(1)}, u32[]{:S(2)}, u32[]{:S(2)}) collective-permute-start(bf16[2,2,2,128,128]{4,3,2,0,1:T(8,128)(2,1)S(1)} %get-tuple-element.1208), channel_id=1, source_target_pairs={{0,32},{32,64},{64,96},{96,128},{128,160},{160,192},{192,224},{224... | collective-permute-start | bytes 786440 | tf_op jit(solution)/shard_map/while/body/eval_jaxpr/ppermute | solution.py:14
  305.7 4.6 collective-permute-done
  317.8 18.0 %collective-permute-start = (bf16[2,2,2,128,128]{4,3,2,0,1:T(8,128)(2,1)S(1)}, bf16[2,2,2,128,128]{4,3,2,0,1:T(8,128)(2,1)S(1)}, u32[]{:S(2)}, u32[]{:S(2)}) collective-permute-start(bf16[2,2,2,128,128]{4,3,2,0,1:T(8,128)(2,1)S(1)} %get-tuple-element.1208), channel_id=1, source_target_pairs={{0,32},{32,64},{64,96},{96,128},{128,160},{160,192},{192,224},{224... | collective-permute-start | bytes 786440 | tf_op jit(solution)/shard_map/while/body/eval_jaxpr/ppermute | solution.py:14
  335.8 4.4 collective-permute-done
  340.2 9.7 conditional.3
  351.1 941.7 %while.42 = (s32[]{:T(128)}, bf16[2,2,2,128,128]{4,3,2,0,1:T(8,128)(2,1)S(1)}, f32[2,2,256,256]{3,2,1,0:T(8,128)}, f32[2,2,128,128]{3,2,1,0:T(8,128)S(1)}, s32[]...) while((s32[]{:T(128)}, ...), condition=%wide.region_15.16_spmd, body=%wide.region_7.15_spmd.sunk | while | flops 1614479360 | bytes 30409676 | solution.py:220
  353.2 6.8 collective-permute-done.1
  362.0 20.5 %collective-permute-done.1 = bf16[2,2,2,128,128]{4,3,2,0,1:T(8,128)(2,1)S(1)} collective-permute-done((bf16[2,2,2,128,128]{4,3,2,0,1:T(8,128)(2,1)}, bf16[2,2,2,128,128]{4,3,2,0,1:T(8,128)(2,1)S(1)}, u32[]{:S(2)}, u32[]{:S(2)}) %collective-permute-start.1) | collective-permute-done | bytes 262176 | tf_op jit(solution)/shard_map/while/body/eval_jaxpr/ppermute | solution.py:14
  384.5 8.0 collective-permute-done.1
  394.6 20.0 %collective-permute-done.1 = bf16[2,2,2,128,128]{4,3,2,0,1:T(8,128)(2,1)S(1)} collective-permute-done((bf16[2,2,2,128,128]{4,3,2,0,1:T(8,128)(2,1)}, bf16[2,2,2,128,128]{4,3,2,0,1:T(8,128)(2,1)S(1)}, u32[]{:S(2)}, u32[]{:S(2)}) %collective-permute-start.1) | collective-permute-done | bytes 262176 | tf_op jit(solution)/shard_map/while/body/eval_jaxpr/ppermute | solution.py:14
  416.6 6.4 collective-permute-done.1
  425.0 19.2 %collective-permute-done.1 = bf16[2,2,2,128,128]{4,3,2,0,1:T(8,128)(2,1)S(1)} collective-permute-done((bf16[2,2,2,128,128]{4,3,2,0,1:T(8,128)(2,1)}, bf16[2,2,2,128,128]{4,3,2,0,1:T(8,128)(2,1)S(1)}, u32[]{:S(2)}, u32[]{:S(2)}) %collective-permute-start.1) | collective-permute-done | bytes 262176 | tf_op jit(solution)/shard_map/while/body/eval_jaxpr/ppermute | solution.py:14
  446.3 7.2 collective-permute-done.1
  455.6 26.3 %collective-permute-done.1 = bf16[2,2,2,128,128]{4,3,2,0,1:T(8,128)(2,1)S(1)} collective-permute-done((bf16[2,2,2,128,128]{4,3,2,0,1:T(8,128)(2,1)}, bf16[2,2,2,128,128]{4,3,2,0,1:T(8,128)(2,1)S(1)}, u32[]{:S(2)}, u32[]{:S(2)}) %collective-permute-start.1) | collective-permute-done | bytes 262176 | tf_op jit(solution)/shard_map/while/body/eval_jaxpr/ppermute | solution.py:14
  483.9 7.2 collective-permute-done.1
  493.2 8.8 collective-permute-done.1
  504.1 12.6 collective-permute-done.1
  518.7 23.5 %collective-permute-done.1 = bf16[2,2,2,128,128]{4,3,2,0,1:T(8,128)(2,1)S(1)} collective-permute-done((bf16[2,2,2,128,128]{4,3,2,0,1:T(8,128)(2,1)}, bf16[2,2,2,128,128]{4,3,2,0,1:T(8,128)(2,1)S(1)}, u32[]{:S(2)}, u32[]{:S(2)}) %collective-permute-start.1) | collective-permute-done | bytes 262176 | tf_op jit(solution)/shard_map/while/body/eval_jaxpr/ppermute | solution.py:14
  544.2 9.6 collective-permute-done.1
  555.9 19.2 %collective-permute-done.1 = bf16[2,2,2,128,128]{4,3,2,0,1:T(8,128)(2,1)S(1)} collective-permute-done((bf16[2,2,2,128,128]{4,3,2,0,1:T(8,128)(2,1)}, bf16[2,2,2,128,128]{4,3,2,0,1:T(8,128)(2,1)S(1)}, u32[]{:S(2)}, u32[]{:S(2)}) %collective-permute-start.1) | collective-permute-done | bytes 262176 | tf_op jit(solution)/shard_map/while/body/eval_jaxpr/ppermute | solution.py:14
  577.1 537.0 %collective-permute-done.1 = bf16[2,2,2,128,128]{4,3,2,0,1:T(8,128)(2,1)S(1)} collective-permute-done((bf16[2,2,2,128,128]{4,3,2,0,1:T(8,128)(2,1)}, bf16[2,2,2,128,128]{4,3,2,0,1:T(8,128)(2,1)S(1)}, u32[]{:S(2)}, u32[]{:S(2)}) %collective-permute-start.1) | collective-permute-done | bytes 262176 | tf_op jit(solution)/shard_map/while/body/eval_jaxpr/ppermute | solution.py:14
  1114.1 35.8 %conditional.7 = (f32[2,2,256,256]{3,2,1,0:T(8,128)}, f32[2,2,128,128]{3,2,1,0:T(8,128)S(1)}, bf16[2,2,2,128,128]{4,3,2,0,1:T(8,128)(2,1)}) conditional(s32[]{:T(128)} %convert_element_type.177, (f32[2,2,256,256]{3,2,1,0:T(8,128)}, f32[2,2,128,128]{3,2,1,0:T(8,128)S(1)}) %tuple.183, (s32[]{:T(128)}, s32[8,2]{1,0:T(8,128)S(1)}, ...), branch_computations={%region_8.8_spmd, %region_9.14_spmd} | conditional | flops 1614479360 | bytes 29360776 | solution.py:209
  1145.6 4.2 dynamic_update_slice.17
  1151.1 8.2 collective-permute-done.1
  1159.3 35.9 %conditional.7 = (f32[2,2,256,256]{3,2,1,0:T(8,128)}, f32[2,2,128,128]{3,2,1,0:T(8,128)S(1)}, bf16[2,2,2,128,128]{4,3,2,0,1:T(8,128)(2,1)}) conditional(s32[]{:T(128)} %convert_element_type.177, (f32[2,2,256,256]{3,2,1,0:T(8,128)}, f32[2,2,128,128]{3,2,1,0:T(8,128)S(1)}) %tuple.183, (s32[]{:T(128)}, s32[8,2]{1,0:T(8,128)S(1)}, ...), branch_computations={%region_8.8_spmd, %region_9.14_spmd} | conditional | flops 1614479360 | bytes 29360776 | solution.py:209
  1181.7 4.2 dynamic_update_slice.16
  1190.9 4.3 dynamic_update_slice.17
  1196.4 7.2 collective-permute-done.1
  1203.6 35.7 %conditional.7 = (f32[2,2,256,256]{3,2,1,0:T(8,128)}, f32[2,2,128,128]{3,2,1,0:T(8,128)S(1)}, bf16[2,2,2,128,128]{4,3,2,0,1:T(8,128)(2,1)}) conditional(s32[]{:T(128)} %convert_element_type.177, (f32[2,2,256,256]{3,2,1,0:T(8,128)}, f32[2,2,128,128]{3,2,1,0:T(8,128)S(1)}) %tuple.183, (s32[]{:T(128)}, s32[8,2]{1,0:T(8,128)S(1)}, ...), branch_computations={%region_8.8_spmd, %region_9.14_spmd} | conditional | flops 1614479360 | bytes 29360776 | solution.py:209
  1240.6 8.9 collective-permute-done.1
  1249.5 35.6 %conditional.7 = (f32[2,2,256,256]{3,2,1,0:T(8,128)}, f32[2,2,128,128]{3,2,1,0:T(8,128)S(1)}, bf16[2,2,2,128,128]{4,3,2,0,1:T(8,128)(2,1)}) conditional(s32[]{:T(128)} %convert_element_type.177, (f32[2,2,256,256]{3,2,1,0:T(8,128)}, f32[2,2,128,128]{3,2,1,0:T(8,128)S(1)}) %tuple.183, (s32[]{:T(128)}, s32[8,2]{1,0:T(8,128)S(1)}, ...), branch_computations={%region_8.8_spmd, %region_9.14_spmd} | conditional | flops 1614479360 | bytes 29360776 | solution.py:209
  1286.4 6.4 collective-permute-done.1
  1293.5 488.4 %all-reduce.3.cloned.1.call-done = f32[65536]{0:T(1024)} async-done(((f32[65536]{0:T(1024)}), f32[65536]{0:T(1024)}) %all-reduce.3.cloned.1.call-update) | async-done | bytes 262160
  (455 shorter events, 334.8 us)
Async XLA Ops:
  7.2 2.4 copy-start.4
  7.2 2.5 copy-start.3
  7.2 1774.7 %all-reduce.3.cloned.1.call-start = ((), (), s32[]{:S(2)}) async-start(), calls=%async_computation | async-start | bytes 524288
  12.1 1.6 copy-start
  13.8 326.4 %copy-start.2 = (bf16[8,128,128]{2,1,0:T(8,128)(2,1)S(1)}, bf16[8,128,128]{2,1,0:T(8,128)(2,1)}, u32[]{:S(2)}) copy-start(bf16[8,128,128]{2,1,0:T(8,128)(2,1)} %param.17) | copy-start | bytes 786436
  30.4 4.6 collective-permute-start
  50.9 7.2 collective-permute-start
  74.1 7.1 collective-permute-start
  97.1 7.1 collective-permute-start
  104.3 23.0 %collective-permute-start = (bf16[2,2,2,128,128]{4,3,2,0,1:T(8,128)(2,1)S(1)}, bf16[2,2,2,128,128]{4,3,2,0,1:T(8,128)(2,1)S(1)}, u32[]{:S(2)}, u32[]{:S(2)}) collective-permute-start(bf16[2,2,2,128,128]{4,3,2,0,1:T(8,128)(2,1)S(1)} %get-tuple-element.1208), channel_id=1, source_target_pairs={{0,32},{32,64},{64,96},{96,128},{128,160},{160,192},{192,224},{224... | collective-permute-start | bytes 786440 | tf_op jit(solution)/shard_map/while/body/eval_jaxpr/ppermute | solution.py:14
  127.4 7.1 collective-permute-start
  134.6 21.2 %collective-permute-start = (bf16[2,2,2,128,128]{4,3,2,0,1:T(8,128)(2,1)S(1)}, bf16[2,2,2,128,128]{4,3,2,0,1:T(8,128)(2,1)S(1)}, u32[]{:S(2)}, u32[]{:S(2)}) collective-permute-start(bf16[2,2,2,128,128]{4,3,2,0,1:T(8,128)(2,1)S(1)} %get-tuple-element.1208), channel_id=1, source_target_pairs={{0,32},{32,64},{64,96},{96,128},{128,160},{160,192},{192,224},{224... | collective-permute-start | bytes 786440 | tf_op jit(solution)/shard_map/while/body/eval_jaxpr/ppermute | solution.py:14
  155.8 7.1 collective-permute-start
  163.0 21.8 %collective-permute-start = (bf16[2,2,2,128,128]{4,3,2,0,1:T(8,128)(2,1)S(1)}, bf16[2,2,2,128,128]{4,3,2,0,1:T(8,128)(2,1)S(1)}, u32[]{:S(2)}, u32[]{:S(2)}) collective-permute-start(bf16[2,2,2,128,128]{4,3,2,0,1:T(8,128)(2,1)S(1)} %get-tuple-element.1208), channel_id=1, source_target_pairs={{0,32},{32,64},{64,96},{96,128},{128,160},{160,192},{192,224},{224... | collective-permute-start | bytes 786440 | tf_op jit(solution)/shard_map/while/body/eval_jaxpr/ppermute | solution.py:14
  184.8 8.4 collective-permute-start
  193.2 24.2 %collective-permute-start = (bf16[2,2,2,128,128]{4,3,2,0,1:T(8,128)(2,1)S(1)}, bf16[2,2,2,128,128]{4,3,2,0,1:T(8,128)(2,1)S(1)}, u32[]{:S(2)}, u32[]{:S(2)}) collective-permute-start(bf16[2,2,2,128,128]{4,3,2,0,1:T(8,128)(2,1)S(1)} %get-tuple-element.1208), channel_id=1, source_target_pairs={{0,32},{32,64},{64,96},{96,128},{128,160},{160,192},{192,224},{224... | collective-permute-start | bytes 786440 | tf_op jit(solution)/shard_map/while/body/eval_jaxpr/ppermute | solution.py:14
  217.5 8.3 collective-permute-start
  225.9 20.7 %collective-permute-start = (bf16[2,2,2,128,128]{4,3,2,0,1:T(8,128)(2,1)S(1)}, bf16[2,2,2,128,128]{4,3,2,0,1:T(8,128)(2,1)S(1)}, u32[]{:S(2)}, u32[]{:S(2)}) collective-permute-start(bf16[2,2,2,128,128]{4,3,2,0,1:T(8,128)(2,1)S(1)} %get-tuple-element.1208), channel_id=1, source_target_pairs={{0,32},{32,64},{64,96},{96,128},{128,160},{160,192},{192,224},{224... | collective-permute-start | bytes 786440 | tf_op jit(solution)/shard_map/while/body/eval_jaxpr/ppermute | solution.py:14
  246.6 7.5 collective-permute-start
  254.2 24.8 %collective-permute-start = (bf16[2,2,2,128,128]{4,3,2,0,1:T(8,128)(2,1)S(1)}, bf16[2,2,2,128,128]{4,3,2,0,1:T(8,128)(2,1)S(1)}, u32[]{:S(2)}, u32[]{:S(2)}) collective-permute-start(bf16[2,2,2,128,128]{4,3,2,0,1:T(8,128)(2,1)S(1)} %get-tuple-element.1208), channel_id=1, source_target_pairs={{0,32},{32,64},{64,96},{96,128},{128,160},{160,192},{192,224},{224... | collective-permute-start | bytes 786440 | tf_op jit(solution)/shard_map/while/body/eval_jaxpr/ppermute | solution.py:14
  279.1 7.1 collective-permute-start
  286.3 24.0 %collective-permute-start = (bf16[2,2,2,128,128]{4,3,2,0,1:T(8,128)(2,1)S(1)}, bf16[2,2,2,128,128]{4,3,2,0,1:T(8,128)(2,1)S(1)}, u32[]{:S(2)}, u32[]{:S(2)}) collective-permute-start(bf16[2,2,2,128,128]{4,3,2,0,1:T(8,128)(2,1)S(1)} %get-tuple-element.1208), channel_id=1, source_target_pairs={{0,32},{32,64},{64,96},{96,128},{128,160},{160,192},{192,224},{224... | collective-permute-start | bytes 786440 | tf_op jit(solution)/shard_map/while/body/eval_jaxpr/ppermute | solution.py:14
  310.4 7.4 collective-permute-start
  317.8 22.4 %collective-permute-start = (bf16[2,2,2,128,128]{4,3,2,0,1:T(8,128)(2,1)S(1)}, bf16[2,2,2,128,128]{4,3,2,0,1:T(8,128)(2,1)S(1)}, u32[]{:S(2)}, u32[]{:S(2)}) collective-permute-start(bf16[2,2,2,128,128]{4,3,2,0,1:T(8,128)(2,1)S(1)} %get-tuple-element.1208), channel_id=1, source_target_pairs={{0,32},{32,64},{64,96},{96,128},{128,160},{160,192},{192,224},{224... | collective-permute-start | bytes 786440 | tf_op jit(solution)/shard_map/while/body/eval_jaxpr/ppermute | solution.py:14
  351.9 8.1 collective-permute-start.1
  360.7 21.8 %collective-permute-start.1 = (bf16[2,2,2,128,128]{4,3,2,0,1:T(8,128)(2,1)}, bf16[2,2,2,128,128]{4,3,2,0,1:T(8,128)(2,1)S(1)}, u32[]{:S(2)}, u32[]{:S(2)}) collective-permute-start(bf16[2,2,2,128,128]{4,3,2,0,1:T(8,128)(2,1)} %get-tuple-element.1194), channel_id=1, source_target_pairs={{32,0},{64,32},{96,64},{128,96},{160,128},{192,160},{224,192},{256... | collective-permute-start | bytes 786440 | tf_op jit(solution)/shard_map/while/body/eval_jaxpr/ppermute | solution.py:14
  383.2 9.3 collective-permute-start.1
  393.3 21.3 %collective-permute-start.1 = (bf16[2,2,2,128,128]{4,3,2,0,1:T(8,128)(2,1)}, bf16[2,2,2,128,128]{4,3,2,0,1:T(8,128)(2,1)S(1)}, u32[]{:S(2)}, u32[]{:S(2)}) collective-permute-start(bf16[2,2,2,128,128]{4,3,2,0,1:T(8,128)(2,1)} %get-tuple-element.1194), channel_id=1, source_target_pairs={{32,0},{64,32},{96,64},{128,96},{160,128},{192,160},{224,192},{256... | collective-permute-start | bytes 786440 | tf_op jit(solution)/shard_map/while/body/eval_jaxpr/ppermute | solution.py:14
  415.3 7.7 collective-permute-start.1
  423.7 20.5 %collective-permute-start.1 = (bf16[2,2,2,128,128]{4,3,2,0,1:T(8,128)(2,1)}, bf16[2,2,2,128,128]{4,3,2,0,1:T(8,128)(2,1)S(1)}, u32[]{:S(2)}, u32[]{:S(2)}) collective-permute-start(bf16[2,2,2,128,128]{4,3,2,0,1:T(8,128)(2,1)} %get-tuple-element.1194), channel_id=1, source_target_pairs={{32,0},{64,32},{96,64},{128,96},{160,128},{192,160},{224,192},{256... | collective-permute-start | bytes 786440 | tf_op jit(solution)/shard_map/while/body/eval_jaxpr/ppermute | solution.py:14
  445.0 8.5 collective-permute-start.1
  454.3 27.6 %collective-permute-start.1 = (bf16[2,2,2,128,128]{4,3,2,0,1:T(8,128)(2,1)}, bf16[2,2,2,128,128]{4,3,2,0,1:T(8,128)(2,1)S(1)}, u32[]{:S(2)}, u32[]{:S(2)}) collective-permute-start(bf16[2,2,2,128,128]{4,3,2,0,1:T(8,128)(2,1)} %get-tuple-element.1194), channel_id=1, source_target_pairs={{32,0},{64,32},{96,64},{128,96},{160,128},{192,160},{224,192},{256... | collective-permute-start | bytes 786440 | tf_op jit(solution)/shard_map/while/body/eval_jaxpr/ppermute | solution.py:14
  482.6 8.5 collective-permute-start.1
  491.9 10.1 collective-permute-start.1
  502.8 13.8 collective-permute-start.1
  517.4 24.8 %collective-permute-start.1 = (bf16[2,2,2,128,128]{4,3,2,0,1:T(8,128)(2,1)}, bf16[2,2,2,128,128]{4,3,2,0,1:T(8,128)(2,1)S(1)}, u32[]{:S(2)}, u32[]{:S(2)}) collective-permute-start(bf16[2,2,2,128,128]{4,3,2,0,1:T(8,128)(2,1)} %get-tuple-element.1194), channel_id=1, source_target_pairs={{32,0},{64,32},{96,64},{128,96},{160,128},{192,160},{224,192},{256... | collective-permute-start | bytes 786440 | tf_op jit(solution)/shard_map/while/body/eval_jaxpr/ppermute | solution.py:14
  542.9 10.9 collective-permute-start.1
  554.6 20.4 %collective-permute-start.1 = (bf16[2,2,2,128,128]{4,3,2,0,1:T(8,128)(2,1)}, bf16[2,2,2,128,128]{4,3,2,0,1:T(8,128)(2,1)S(1)}, u32[]{:S(2)}, u32[]{:S(2)}) collective-permute-start(bf16[2,2,2,128,128]{4,3,2,0,1:T(8,128)(2,1)} %get-tuple-element.1194), channel_id=1, source_target_pairs={{32,0},{64,32},{96,64},{128,96},{160,128},{192,160},{224,192},{256... | collective-permute-start | bytes 786440 | tf_op jit(solution)/shard_map/while/body/eval_jaxpr/ppermute | solution.py:14
  575.8 538.3 %collective-permute-start.1 = (bf16[2,2,2,128,128]{4,3,2,0,1:T(8,128)(2,1)}, bf16[2,2,2,128,128]{4,3,2,0,1:T(8,128)(2,1)S(1)}, u32[]{:S(2)}, u32[]{:S(2)}) collective-permute-start(bf16[2,2,2,128,128]{4,3,2,0,1:T(8,128)(2,1)} %get-tuple-element.1194), channel_id=1, source_target_pairs={{32,0},{64,32},{96,64},{128,96},{160,128},{192,160},{224,192},{256... | collective-permute-start | bytes 786440 | tf_op jit(solution)/shard_map/while/body/eval_jaxpr/ppermute | solution.py:14
  1149.8 9.5 collective-permute-start.1
  1195.2 8.5 collective-permute-start.1
  1239.3 10.2 collective-permute-start.1
  1285.1 7.7 collective-permute-start.1
Sparse Core Ops, SparseCore 0:
  1293.6 488.2 all-reduce.2
where the time goes:
time: 1800 us; the launch traced here: 1790 us
  waiting for transfers between devices  1320 us (73%)
  starting transfers between devices  217 us (12%)
  local copies, waits for them, and re-layouts  94.1 us (5%)
  matrix products  75 us (4%)
  loops' own time  41.7 us (2%)
  other arithmetic  28.3 us (2%)
    ppermute x38, waiting for transfers between devices, from_behind(): lax.ppermute(value, axis, [(source, source + steps) for source in range(l...  831 us
    unnamed x2, waiting for transfers between devices  488 us
    ppermute x38, starting transfers between devices, from_behind(): lax.ppermute(value, axis, [(source, source + steps) for source in range(l...  217 us
    dot_general x64, matrix products, right_apply(): jnp.einsum('bmcd,de->bmce', field_in, matrix_in, precision=lax.Precision....  38.4 us
  transfers between devices with their start and end apart: 39, of which 39 were waited for; matrix products, arithmetic and copies ran while one was open for 0% of the time, Pallas kernels for 0%

commit v1 on v0

v1 whole, which is shorter than its diff:
```python
import functools

import jax
import jax.numpy as jnp
import ml_dtypes
import numpy as np
from jax import lax
from jax.experimental import pallas as pl
from jax.experimental.pallas import tpu as pltpu
from jax.sharding import PartitionSpec as P

PHASE_SCALE = 20.0
F32 = jnp.float32
BF16 = jnp.bfloat16
MESH = pl.DeviceIdType.MESH


def real_forms(matrix):
    re, im = matrix.real, matrix.imag
    left = np.block([[re, -im], [im, re]])
    right = np.block([[re, im], [-im, re]])
    pieces = []
    for table in (right, left):
        table = table.astype(np.float32)
        high = table.astype(ml_dtypes.bfloat16)
        low = (table - high.astype(np.float32)).astype(ml_dtypes.bfloat16)
        pieces += [high, low]
    return pieces


def tables(length):
    index = np.arange(length)
    dft = np.exp(-2j * np.pi * (np.outer(index, index) % length) / length)
    frequency = np.where(index < (length + 1) // 2, index, index - length) / length
    phases = np.exp(-1j * PHASE_SCALE * frequency * frequency)
    propagator = (dft.conj() @ (phases[:, None] * dft)) / length
    return np.stack(real_forms(propagator) + real_forms(dft / np.sqrt(length)))


def split(value):
    high = value.astype(BF16)
    return high, (value - high.astype(F32)).astype(BF16)


def dot(a, b):
    return jnp.dot(a, b, preferred_element_type=F32)


def two_sided(tab_ref, right, left, re, im):
    n = re.shape[0]
    high, low = split(jnp.concatenate([re, im], axis=1))
    right_high = tab_ref[right]
    half = dot(high, right_high) + dot(low, right_high) + dot(high, tab_ref[right + 1])
    high, low = split(jnp.concatenate([half[:, :n], half[:, n:]], axis=0))
    both = dot(tab_ref[left], jnp.concatenate([high, low], axis=1))
    out = both[:, :n] + both[:, n:] + dot(tab_ref[left + 1], high)
    return out[:n], out[n:]


def one_hot(rows, columns, row_shift, column_shift):
    down = lax.broadcasted_iota(jnp.int32, (rows, columns), 0) + row_shift
    across = lax.broadcasted_iota(jnp.int32, (rows, columns), 1) + column_shift
    return jnp.where(down == across, 1.0, 0.0).astype(BF16)


def kernel(
    sections, tiles,
    slab_ref, probe_ref, amps_ref, offsets_ref, counts_ref, tab_ref,
    grad_ref, probe_out_ref,
    slab_parts, win, entering, mid, exits, seeds, patch, probe_acc,
    send_f, recv_f, send_b, recv_b, pieces, sums,
    sem_sf, sem_rf, sem_sb, sem_rb, sem_ps, sem_pr, sem_zs, sem_zr,
):
    n = probe_ref.shape[-1]
    tile_side = slab_ref.shape[-1]
    layers = slab_ref.shape[0]
    waves = send_f.shape[0]
    positions = waves // 2
    s = lax.axis_index("sec")
    t = lax.axis_index("tile")
    first, last = s == 0, s == sections - 1
    planes = [(l, c) for l in range(layers) for c in range(2)]

    barrier = pltpu.get_barrier_semaphore()

    def greet(sec, tile):
        pl.semaphore_signal(barrier, inc=1, device_id=(sec, tile), device_id_type=MESH)

    @pl.when(first)
    def _():
        greet(1, t)
        for other in range(tiles):
            @pl.when(other != t)
            def _():
                greet(0, other)

    @pl.when(s > 0)
    def _():
        greet(s - 1, t)

        @pl.when(s > 1)
        def _():
            greet(0, t)

        @pl.when(s < sections - 1)
        def _():
            greet(s + 1, t)

    for at, (l, c) in enumerate(planes):
        high, low = split(slab_ref[l, c])
        slab_parts[:, at * tile_side:(at + 1) * tile_side] = high
        shift = (at + len(planes)) * tile_side
        slab_parts[:, shift:shift + tile_side] = low
    grad_ref[...] = jnp.zeros_like(grad_ref)
    patch[...] = jnp.zeros_like(patch)
    probe_acc[...] = jnp.zeros_like(probe_acc)

    def cut(p):
        rows = one_hot(n, tile_side, offsets_ref[p, 0], 0)
        columns = one_hot(tile_side, n, 0, offsets_ref[p, 1])
        for at, (l, c) in enumerate(planes):
            value = None
            for part in (at, at + len(planes)):
                strip = dot(rows, slab_parts[:, part * tile_side:(part + 1) * tile_side]).astype(BF16)
                term = dot(strip, columns)
                value = term if value is None else value + term
            win[p, l, c] = value

    def place(p):
        rows = one_hot(tile_side, n, 0, offsets_ref[p, 0])
        columns = one_hot(n, tile_side, offsets_ref[p, 1], 0)
        for l, c in planes:
            high, low = split(patch[l, c])
            wide = jnp.concatenate([dot(high, columns).astype(BF16), dot(low, columns).astype(BF16)], axis=1)
            both = dot(rows, wide)
            grad_ref[l, c] += both[:, :tile_side] + both[:, tile_side:]
        patch[...] = jnp.zeros_like(patch)

    def copy_f(k):
        return pltpu.make_async_remote_copy(
            src_ref=send_f.at[k], dst_ref=recv_f.at[k], send_sem=sem_sf.at[k], recv_sem=sem_rf.at[k],
            device_id=(s + 1, t), device_id_type=MESH)

    def copy_b(k):
        return pltpu.make_async_remote_copy(
            src_ref=send_b.at[k], dst_ref=recv_b.at[k], send_sem=sem_sb.at[k], recv_sem=sem_rb.at[k],
            device_id=(s - 1, t), device_id_type=MESH)

    cut(0)

    @pl.when(first)
    def _():
        pl.semaphore_wait(barrier, sections - 1 + tiles - 1)

    @pl.when((s > 0) & (s < sections - 1))
    def _():
        pl.semaphore_wait(barrier, 2)

    @pl.when(last)
    def _():
        pl.semaphore_wait(barrier, 1)

    def forward(k):
        p, m = k // 2, k % 2

        @pl.when(first)
        def _():
            entering[...] = probe_ref[m]

        @pl.when(s > 0)
        def _():
            copy_f(k).wait_recv()
            entering[...] = recv_f[k].astype(F32)

        re, im = entering[0], entering[1]
        for l in range(layers):
            if l > 0:
                mid[k, 0] = re
                mid[k, 1] = im
            tr, ti = win[p, l, 0], win[p, l, 1]
            re, im = two_sided(tab_ref, 0, 2, tr * re - ti * im, tr * im + ti * re)
        send_f[k, 0] = re.astype(BF16)
        send_f[k, 1] = im.astype(BF16)

        @pl.when(s < sections - 1)
        def _():
            copy_f(k).start()

        exits[m, 0] = re
        exits[m, 1] = im

    def far(p):
        spectrum = [two_sided(tab_ref, 4, 6, exits[m, 0], exits[m, 1]) for m in range(2)]
        intensity = sum(re * re + im * im for re, im in spectrum)
        modelled = jnp.sqrt(intensity + 0.25)
        live = jnp.where(p < counts_ref[0], 2.0, 0.0)
        factor = live * (1.0 - amps_ref[p].astype(F32) / modelled)
        for m, (re, im) in enumerate(spectrum):
            seeds[m, 0], seeds[m, 1] = two_sided(tab_ref, 6, 4, factor * re, factor * im)

    def backward(k):
        p, m = k // 2, k % 2

        @pl.when(last)
        def _():
            entering[...] = seeds[m]

        @pl.when(s < sections - 1)
        def _():
            copy_b(k).wait_recv()
            entering[...] = recv_b[k].astype(F32)

        re, im = entering[0], entering[1]

        @pl.when(first)
        def _():
            entering[...] = probe_ref[m]

        @pl.when(s > 0)
        def _():
            entering[...] = recv_f[k].astype(F32)

        for l in reversed(range(layers)):
            re, im = two_sided(tab_ref, 2, 0, re, im)
            xr, xi = (entering[0], entering[1]) if l == 0 else (mid[k, 0], mid[k, 1])
            patch[l, 0] += xr * re + xi * im
            patch[l, 1] += xr * im - xi * re
            tr, ti = win[p, l, 0], win[p, l, 1]
            re, im = tr * re + ti * im, tr * im - ti * re
        send_b[k, 0] = re.astype(BF16)
        send_b[k, 1] = im.astype(BF16)

        @pl.when(s > 0)
        def _():
            copy_b(k).start()

        @pl.when(first)
        def _():
            groups = sections // 4
            for c, part in enumerate((re, im)):
                where = pl.ds((2 * m + c) * groups, groups)
                probe_acc[where] += part.reshape((groups,) + probe_acc.shape[1:])

        @pl.when(m == 1)
        def _():
            place(p)

    lag = jnp.minimum(waves, 2 + 5 * (sections - 1 - s))

    def turn(k, carry):
        @pl.when((k >= lag) & (k < lag + waves))
        def _():
            backward(k - lag)

        @pl.when(k < waves)
        def _():
            forward(k)

            @pl.when(last & (k % 2 == 1))
            def _():
                far(k // 2)

            @pl.when((k % 2 == 0) & (k < waves - 2))
            def _():
                cut(k // 2 + 1)

        return carry

    lax.fori_loop(0, 2 * waves, turn, 0)

    share = probe_acc.shape[1] // tiles

    def of_tile(other):
        return probe_acc.at[:, other] if share == 1 else probe_acc.at[:, pl.ds(other * share, share)]

    def copy_p(other):
        return pltpu.make_async_remote_copy(
            src_ref=of_tile(other), dst_ref=pieces.at[t], send_sem=sem_ps.at[other], recv_sem=sem_pr.at[t],
            device_id=(0, other), device_id_type=MESH)

    def arrival_p(other):
        return pltpu.make_async_remote_copy(
            src_ref=of_tile(0), dst_ref=pieces.at[other], send_sem=sem_ps.at[other], recv_sem=sem_pr.at[other],
            device_id=(0, other), device_id_type=MESH)

    def copy_z(sec):
        return pltpu.make_async_remote_copy(
            src_ref=sums.at[sec], dst_ref=sums.at[0], send_sem=sem_zs.at[sec], recv_sem=sem_zr,
            device_id=(sec, t), device_id_type=MESH)

    @pl.when(first)
    def _():
        for other in range(tiles):
            @pl.when(other != t)
            def _():
                copy_p(other).start()

            @pl.when(other == t)
            def _():
                pieces[other] = of_tile(other)[...]
        for other in range(tiles):
            @pl.when(other != t)
            def _():
                arrival_p(other).wait_recv()
        total = pieces[0]
        for other in range(1, tiles):
            total = total + pieces[other]
        for sec in range(sections):
            sums[sec] = jnp.broadcast_to(total[sec], sums.shape[1:])
        for sec in range(1, sections):
            copy_z(sec).start()
        for other in range(tiles):
            @pl.when(other != t)
            def _():
                copy_p(other).wait_send()
        for sec in range(1, sections):
            copy_z(sec).wait_send()

    @pl.when(s > 0)
    def _():
        copy_z(s).wait_recv()

    probe_out_ref[...] = sums[0]

    for k in range(waves):
        @pl.when(s < sections - 1)
        def _():
            copy_f(k).wait_send()

        @pl.when(s > 0)
        def _():
            copy_b(k).wait_send()


def shards(sections, tiles, slab, probe, amplitudes, offsets, counts):
    layers, _, side, _ = slab.shape
    n = probe.shape[-1]
    waves = offsets.shape[0] * 2
    lines = 4 * n // sections
    share = lines // tiles
    piece = (sections, n) if share == 1 else (sections, share, n)
    sum_rows = max(8, share)
    vmem = pl.BlockSpec(memory_space=pltpu.VMEM)
    smem = pl.BlockSpec(memory_space=pltpu.SMEM)
    wave = (waves, 2, n, n)
    grad, probe_grad = pl.pallas_call(
        functools.partial(kernel, sections, tiles),
        out_shape=(
            jax.ShapeDtypeStruct(slab.shape, F32),
            jax.ShapeDtypeStruct((sum_rows, n), F32),
        ),
        in_specs=[vmem, vmem, vmem, smem, smem, vmem],
        out_specs=(vmem, vmem),
        scratch_shapes=[
            pltpu.VMEM((side, side * layers * 4), BF16),
            pltpu.VMEM((waves // 2, layers, 2, n, n), F32),
            pltpu.VMEM((2, n, n), F32),
            pltpu.VMEM(wave, F32),
            pltpu.VMEM((2, 2, n, n), F32),
            pltpu.VMEM((2, 2, n, n), F32),
            pltpu.VMEM((layers, 2, n, n), F32),
            pltpu.VMEM((sections, lines, n), F32),
            pltpu.VMEM(wave, BF16),
            pltpu.VMEM(wave, BF16),
            pltpu.VMEM(wave, BF16),
            pltpu.VMEM(wave, BF16),
            pltpu.VMEM((tiles,) + piece, F32),
            pltpu.VMEM((sections, sum_rows, n), F32),
            pltpu.SemaphoreType.DMA((waves,)),
            pltpu.SemaphoreType.DMA((waves,)),
            pltpu.SemaphoreType.DMA((waves,)),
            pltpu.SemaphoreType.DMA((waves,)),
            pltpu.SemaphoreType.DMA((tiles,)),
            pltpu.SemaphoreType.DMA((tiles,)),
            pltpu.SemaphoreType.DMA((sections,)),
            pltpu.SemaphoreType.DMA,
        ],
        compiler_params=pltpu.CompilerParams(
            collective_id=0, has_side_effects=True, vmem_limit_bytes=48 * 1024 * 1024),
    )(slab, probe, amplitudes, offsets, counts, jnp.asarray(tables(n)))
    return grad, probe_grad[:share].reshape(-1)


def solution(mesh):
    body = functools.partial(shards, mesh.shape["sec"], mesh.shape["tile"])
    in_specs = (
        P("sec", None, "tile", None),
        P(),
        P("tile", None, None),
        P("tile", None),
        P("tile"),
    )
    out_specs = (P("sec", None, "tile", None), P(("sec", "tile")))
    return jax.shard_map(body, mesh=mesh, in_specs=in_specs, out_specs=out_specs, check_vma=False)
```

time: 1800 us -> 221 us (0.12)
  waiting for transfers between devices: 1320 us -> 0 us
  starting transfers between devices: 217 us -> 0 us
  Pallas kernels: 0 us -> 214 us
  local copies, waits for them, and re-layouts: 94.1 us -> 5.92 us
  matrix products: 75 us -> 0 us
  loops' own time: 41.7 us -> 0 us
  other arithmetic: 28.3 us -> 0 us
    ppermute x38 -> x0, waiting for transfers between devices: 831 us -> none  [from_behind(): lax.ppermute(value, axis, [(source, source + steps) for source in range(l...]
    unnamed x2 -> x0, waiting for transfers between devices: 488 us -> none
    ppermute x38 -> x0, starting transfers between devices: 217 us -> none  [from_behind(): lax.ppermute(value, axis, [(source, source + steps) for source in range(l...]
    pallas_call x0 -> x1, Pallas kernels: none -> 214 us  [shards(): pl.pallas_call(functools.partial(kernel, sections, tiles), out_shape=(jax...]
    dot_general x132 -> x0, matrix products: 75 us -> none  [the longest x64 38.4 us: right_apply(): jnp.einsum('bmcd,de->bmce', field_in, matrix_in, precision=lax.Precision....]
    another operation x49 -> x0, loops' own time: 41.7 us -> none  [the longest x19 31.2 us: backward_turn(): lax.cond(active, backward_compute_block, backward_skip_block, (slab_grad,...]
    dynamic_update_slice x8 -> x0, local copies, waits for them, and re-layouts: 33.4 us -> none  [backward_compute_block(): lax.dynamic_update_slice(accumulated, current + patch_grads[member], corner)]
    gather x48 -> x0, local copies, waits for them, and re-layouts: 31.8 us -> none
  transfers between devices with their start and end apart: 39 -> 0, of which waited for: 39 -> 0; matrix products, arithmetic and copies ran while one was open for 0% -> 0% of each run, Pallas kernels for 0% -> 0%
where the time goes in v1:
time: 221 us
  Pallas kernels  214 us (97%)
  local copies, waits for them, and re-layouts  5.92 us (3%)
    pallas_call x1, Pallas kernels, shards(): pl.pallas_call(functools.partial(kernel, sections, tiles), out_shape=(jax...  214 us
    unnamed x12, local copies, waits for them, and re-layouts  5.41 us

profile of v1, /device:TPU:1, one launch (start us, length us, event | category | flops | bytes accessed | tf_op | source)
XLA Modules:
  0.0 220.7 jit_solution(2522075155625674163)
XLA Ops:
  0.6 0.0 copy-start.4
  1.3 0.0 copy-done.4
  1.3 0.1 copy.8.offsets_ref
  1.4 0.0 copy-start
  1.4 1.2 copy-done
  2.6 0.0 copy-start.1
  2.6 1.2 copy-done.1
  3.8 0.0 copy-start.2
  3.8 0.9 copy-done.2
  4.8 0.0 copy-start.3
  4.8 0.9 copy-done.3
  5.7 213.5 %shard_map.77 = (f32[2,2,256,256]{3,2,1,0:T(8,128)S(1)}, f32[8,128]{1,0:T(8,128)S(1)}) custom-call(f32[2,2,256,256]{3,2,1,0:T(8,128)S(1)} %copy-done, f32[2,2,128,128]{3,2,1,0:T(8,128)S(1)} %copy-done.2, bf16[8,128,128]{2,1,0:T(8,128)(2,1)S(1)} %copy-done.3, s32[8,2]{1,0:T(8,128)S(1)} %copy.8.offsets_ref, s32[1]{0:T(128)S(6)} %copy.10.counts_ref, ...), custom_call_target="tpu_custom_call" | custom-call | tf_op jit(solution)/shard_map/pallas_call | solution.py:346
  219.3 0.5 slice_bitcast_fusion
  219.8 1.0 copy.11
Async XLA Ops:
  0.6 0.7 copy-start.4
  1.4 1.2 copy-start
  2.6 1.2 copy-start.1
  3.8 0.9 copy-start.2
  4.8 0.9 copy-start.3

commit v2 on v1

v2 whole, which is shorter than its diff:
```python
import functools

import jax
import jax.numpy as jnp
import ml_dtypes
import numpy as np
from jax import lax
from jax.experimental import pallas as pl
from jax.experimental.pallas import tpu as pltpu
from jax.sharding import PartitionSpec as P

PHASE_SCALE = 20.0
F32 = jnp.float32
BF16 = jnp.bfloat16
MESH = pl.DeviceIdType.MESH


def real_forms(matrix):
    re, im = matrix.real, matrix.imag
    left = np.block([[re, -im], [im, re]])
    right = np.block([[re, im], [-im, re]])
    pieces = []
    for table in (right, left):
        table = table.astype(np.float32)
        high = table.astype(ml_dtypes.bfloat16)
        low = (table - high.astype(np.float32)).astype(ml_dtypes.bfloat16)
        pieces += [high, low]
    return pieces


def tables(length):
    index = np.arange(length)
    dft = np.exp(-2j * np.pi * (np.outer(index, index) % length) / length)
    frequency = np.where(index < (length + 1) // 2, index, index - length) / length
    phases = np.exp(-1j * PHASE_SCALE * frequency * frequency)
    propagator = (dft.conj() @ (phases[:, None] * dft)) / length
    return np.stack(real_forms(propagator) + real_forms(dft / np.sqrt(length)))


def split(value):
    high = value.astype(BF16)
    return high, (value - high.astype(F32)).astype(BF16)


def dot(a, b):
    return jnp.dot(a, b, preferred_element_type=F32)


def two_sided(tab_ref, right, left, re, im):
    n = re.shape[0]
    high, low = split(jnp.concatenate([re, im], axis=1))
    right_high = tab_ref[right]
    half = dot(high, right_high) + dot(low, right_high) + dot(high, tab_ref[right + 1])
    high, low = split(jnp.concatenate([half[:, :n], half[:, n:]], axis=0))
    both = dot(tab_ref[left], jnp.concatenate([high, low], axis=1))
    out = both[:, :n] + both[:, n:] + dot(tab_ref[left + 1], high)
    return out[:n], out[n:]


def one_hot(rows, columns, row_shift, column_shift):
    down = lax.broadcasted_iota(jnp.int32, (rows, columns), 0) + row_shift
    across = lax.broadcasted_iota(jnp.int32, (rows, columns), 1) + column_shift
    return jnp.where(down == across, 1.0, 0.0).astype(BF16)


def by_section(section, values):
    picked = values[0]
    for at in range(1, len(values)):
        if values[at] != values[at - 1]:
            picked = jnp.where(section >= at, values[at], picked)
    return picked


def kernel(
    sizes, tiles,
    slab_hbm, probe_hbm, amps_hbm, offsets_ref, counts_ref, tab_hbm,
    grad_ref, probe_out_ref,
    slab_ref, probe_ref, amps_ref, tab_ref,
    slab_parts, win, win_b, send_w, fields, cur, patch, send_g, recv_g, probe_acc,
    send_f, recv_f, send_b, recv_b, pieces, sums,
    sem_in, sem_sw, sem_rw, sem_sg, sem_rg, sem_sf, sem_rf, sem_sb, sem_rb, sem_ps, sem_pr, sem_zs, sem_zr, sem_go,
):
    n = probe_ref.shape[-1]
    side = slab_ref.shape[-1]
    slots = recv_g.shape[0]
    sections = sum(sizes)
    s = lax.axis_index("sec")
    t = lax.axis_index("tile")
    starts = [sum(sizes[:k]) for k in range(len(sizes))]
    group_of = [k for k, size in enumerate(sizes) for _ in range(size)]
    final = len(sizes) - 1
    size = by_section(s, [sizes[k] for k in group_of])
    start = by_section(s, [starts[k] for k in group_of])
    size_before = by_section(s, [sizes[max(k - 1, 0)] for k in group_of])
    start_before = by_section(s, [starts[max(k - 1, 0)] for k in group_of])
    size_after = by_section(s, [sizes[min(k + 1, final)] for k in group_of])
    start_after = by_section(s, [starts[min(k + 1, final)] for k in group_of])
    links_before = by_section(s, [max(1, sizes[max(k - 1, 0)] // sizes[k]) for k in group_of])
    links_after = by_section(s, [max(1, sizes[min(k + 1, final)] // sizes[k]) for k in group_of])
    rounds = by_section(s, [slots // sizes[k] for k in group_of])
    j = s - start
    first, last = s < starts[1], s >= starts[final]
    heads = sizes[0]

    inputs = [
        pltpu.make_async_copy(source, target, sem_in.at[at])
        for at, (source, target) in enumerate(
            ((slab_hbm, slab_ref), (tab_hbm, tab_ref), (probe_hbm, probe_ref), (amps_hbm, amps_ref)))
    ]
    for copy in inputs:
        copy.start()

    barrier = pltpu.get_barrier_semaphore()

    def greet(sec, tile):
        pl.semaphore_signal(barrier, inc=1, device_id=(sec, tile), device_id_type=MESH)

    for other in range(max(sizes)):
        @pl.when((other < size) & (other != j))
        def _():
            greet(start + other, t)

        @pl.when(jnp.logical_not(first) & (other < links_before))
        def _():
            greet(start_before + (j + size * other) % size_before, t)

        @pl.when(jnp.logical_not(last) & (other < links_after))
        def _():
            greet(start_after + (j + size * other) % size_after, t)

    near_zero = first | ((start == starts[1]) & (j % heads == 0))

    @pl.when(jnp.logical_not(near_zero))
    def _():
        greet(0, t)

    @pl.when(s == 0)
    def _():
        def greet_tile(step, carry):
            for member in range(heads):
                greet(member, (t + step) % tiles)
            return carry

        lax.fori_loop(1, tiles, greet_tile, 0)

    greetings = size - 1
    greetings += jnp.where(first, 0, links_before) + jnp.where(last, 0, links_after)
    greetings += jnp.where(first, tiles - 1, 0)
    greetings += jnp.where(s == 0, sections - heads - max(1, sizes[1] // heads), 0)

    grad_ref[...] = jnp.zeros_like(grad_ref)
    probe_acc[...] = jnp.zeros_like(probe_acc)

    planes = [(l, c) for l in range(2) for c in range(2)]
    inputs[0].wait()
    for at, (l, c) in enumerate(planes):
        high, low = split(slab_ref[l, c])
        slab_parts[:, at * side:(at + 1) * side] = high
        shift = (at + len(planes)) * side
        slab_parts[:, shift:shift + side] = low

    def cut(p, target):
        rows = one_hot(n, side, offsets_ref[p, 0], 0)
        columns = one_hot(side, n, 0, offsets_ref[p, 1])
        for at, (l, c) in enumerate(planes):
            value = None
            for part in (at, at + len(planes)):
                strip = dot(rows, slab_parts[:, part * side:(part + 1) * side]).astype(BF16)
                term = dot(strip, columns)
                value = term if value is None else value + term
            target[l, c] = value.astype(target.dtype)

    def place(p):
        rows = one_hot(side, n, 0, offsets_ref[p, 0])
        columns = one_hot(n, side, offsets_ref[p, 1], 0)
        for l, c in planes:
            strip = dot(recv_g[p, l, c], columns).astype(BF16)
            grad_ref[l, c] += dot(rows, strip)

    def copy_w(p):
        return pltpu.make_async_remote_copy(
            src_ref=send_w.at[p], dst_ref=win_b.at[(p // size) * size + j], send_sem=sem_sw.at[p],
            recv_sem=sem_rw.at[(p // size) * size + j], device_id=(start + p % size, t), device_id_type=MESH)

    def window_arrival(pair, owner):
        return pltpu.make_async_remote_copy(
            src_ref=send_w.at[0], dst_ref=win_b.at[pair], send_sem=sem_sw.at[0],
            recv_sem=sem_rw.at[pair], device_id=(start + owner, t), device_id_type=MESH)

    def copy_g(p, owner):
        pair = (p // size) * size + owner
        return pltpu.make_async_remote_copy(
            src_ref=send_g.at[pair], dst_ref=recv_g.at[p], send_sem=sem_sg.at[pair],
            recv_sem=sem_rg.at[p], device_id=(start + owner, t), device_id_type=MESH)

    def copy_f(p, m):
        return pltpu.make_async_remote_copy(
            src_ref=send_f.at[p, m], dst_ref=recv_f.at[p, m], send_sem=sem_sf.at[p, m], recv_sem=sem_rf.at[p, m],
            device_id=(start_after + p % size_after, t), device_id_type=MESH)

    def copy_b(p, m):
        return pltpu.make_async_remote_copy(
            src_ref=send_b.at[p, m], dst_ref=recv_b.at[p, m], send_sem=sem_sb.at[p, m], recv_sem=sem_rb.at[p, m],
            device_id=(start_before + p % size_before, t), device_id_type=MESH)

    def cut_round(i):
        def one(step, carry):
            member = (j + step) % size
            p = i * size + member

            @pl.when(step < size)
            def _():
                cut(p, send_w.at[p])
                copy_w(p).start()

            @pl.when(step == size)
            def _():
                cut(p, win.at[i * size + j])

            return carry

        lax.fori_loop(1, size + 1, one, 0)

    pl.semaphore_wait(barrier, greetings)
    cut_round(0)

    @pl.when(rounds > 1)
    def _():
        cut_round(1)

    for copy in inputs[1:]:
        copy.wait()

    def forward(i):
        p = i * size + j
        base = i * size * 2

        @pl.when(first)
        def _():
            for m in range(2):
                fields[base, m] = probe_ref[m]

        @pl.when(jnp.logical_not(first))
        def _():
            for m in range(2):
                copy_f(p, m).wait_recv()
                fields[base, m] = recv_f[p, m].astype(F32)

        def slices(owner, carry):
            @pl.when(owner != j)
            def _():
                pair = i * size + owner
                window_arrival(pair, owner).wait_recv()
                win[pair] = win_b[pair].astype(F32)

            for half in range(2):
                at = base + 2 * owner + half
                tr, ti = win[i * size + owner, half, 0], win[i * size + owner, half, 1]
                results = []
                for m in range(2):
                    re, im = fields[at, m, 0], fields[at, m, 1]
                    results.append(two_sided(tab_ref, 0, 2, tr * re - ti * im, tr * im + ti * re))
                for m in range(2):
                    fields[at + 1, m, 0], fields[at + 1, m, 1] = results[m]
            return carry

        lax.fori_loop(0, size, slices, 0)
        end = base + 2 * size

        @pl.when(jnp.logical_not(last))
        def _():
            for m in range(2):
                send_f[p, m] = fields[end, m].astype(BF16)
                copy_f(p, m).start()

        @pl.when(last)
        def _():
            far(p, end)

    def far(p, end):
        spectrum = [two_sided(tab_ref, 4, 6, fields[end, m, 0], fields[end, m, 1]) for m in range(2)]
        intensity = sum(re * re + im * im for re, im in spectrum)
        modelled = jnp.sqrt(intensity + 0.25)
        live = jnp.where(p < counts_ref[0], 2.0, 0.0)
        factor = live * (1.0 - amps_ref[p].astype(F32) / modelled)
        for m, (re, im) in enumerate(spectrum):
            cur[m, 0], cur[m, 1] = two_sided(tab_ref, 6, 4, factor * re, factor * im)

    def backward(i):
        p = i * size + j
        base = i * size * 2

        @pl.when(jnp.logical_not(last))
        def _():
            for m in range(2):
                copy_b(p, m).wait_recv()
                cur[m] = recv_b[p, m].astype(F32)

        def slices(step, carry):
            owner = size - 1 - step
            for half in (1, 0):
                at = base + 2 * owner + half
                tr, ti = win[i * size + owner, half, 0], win[i * size + owner, half, 1]
                middle = [two_sided(tab_ref, 2, 0, cur[m, 0], cur[m, 1]) for m in range(2)]
                piece_re = piece_im = 0.0
                for m, (re, im) in enumerate(middle):
                    xr, xi = fields[at, m, 0], fields[at, m, 1]
                    piece_re += xr * re + xi * im
                    piece_im += xr * im - xi * re
                    cur[m, 0] = tr * re + ti * im
                    cur[m, 1] = tr * im - ti * re
                patch[half, 0] = piece_re.astype(BF16)
                patch[half, 1] = piece_im.astype(BF16)

            @pl.when(owner == j)
            def _():
                recv_g[p] = patch[...]

            @pl.when(owner != j)
            def _():
                send_g[i * size + owner] = patch[...]

                @pl.when(first)
                def _():
                    copy_g(p, owner).start()

            return carry

        lax.fori_loop(0, size, slices, 0)

        @pl.when(jnp.logical_not(first))
        def _():
            for m in range(2):
                send_b[p, m] = cur[m].astype(BF16)
                copy_b(p, m).start()

        @pl.when(first)
        def _():
            groups = sections // 4
            for m in range(2):
                for c in range(2):
                    where = pl.ds((2 * m + c) * groups, groups)
                    probe_acc[where] += cur[m, c].reshape((groups,) + probe_acc.shape[1:])

    def send_patches():
        @pl.when(j == size - 1)
        def _():
            for m in range(2):
                copy_b((rounds - 1) * size + j, m).wait_send()

            def allow(step, carry):
                pl.semaphore_signal(sem_go, inc=1, device_id=(start + step, t), device_id_type=MESH)
                return carry

            lax.fori_loop(0, size - 1, allow, 0)

        @pl.when(j < size - 1)
        def _():
            pl.semaphore_wait(sem_go, 1)

        def of_round(i, carry):
            def one(step, inner):
                copy_g(i * size + j, (j + step) % size).start()
                return inner

            return lax.fori_loop(1, size, one, carry)

        lax.fori_loop(0, rounds, of_round, 0)

    def place_round(i):
        def one(step, carry):
            member = (j + step) % size
            p = i * size + member

            @pl.when(step > 0)
            def _():
                pltpu.make_async_remote_copy(
                    src_ref=send_g.at[0], dst_ref=recv_g.at[p], send_sem=sem_sg.at[0],
                    recv_sem=sem_rg.at[p], device_id=(start + member, t), device_id_type=MESH).wait_recv()

            place(p)
            return carry

        lax.fori_loop(0, size, one, 0)

    def turn(u, carry):
        onward = jnp.where(last, u % 2 == 0, u < rounds)

        @pl.when(onward)
        def _():
            i = jnp.where(last, u // 2, u)
            forward(i)

            @pl.when(i + 2 < rounds)
            def _():
                cut_round(i + 2)

        @pl.when(jnp.logical_not(onward))
        def _():
            i = jnp.where(last, u // 2, u - rounds)
            backward(i)

            @pl.when(first & (i > 0))
            def _():
                place_round(i - 1)

        return carry

    lax.fori_loop(0, 2 * rounds, turn, 0)

    share = probe_acc.shape[1] // tiles

    def of_tile(other):
        return probe_acc.at[:, other] if share == 1 else probe_acc.at[:, pl.ds(other * share, share)]

    def copy_p(other):
        return pltpu.make_async_remote_copy(
            src_ref=of_tile(other), dst_ref=pieces.at[j * tiles + t], send_sem=sem_ps.at[other],
            recv_sem=sem_pr.at[j * tiles + t], device_id=(0, other), device_id_type=MESH)

    def arrival_p(slot):
        return pltpu.make_async_remote_copy(
            src_ref=of_tile(0), dst_ref=pieces.at[slot], send_sem=sem_ps.at[0], recv_sem=sem_pr.at[slot],
            device_id=(0, t), device_id_type=MESH)

    def copy_z(sec):
        return pltpu.make_async_remote_copy(
            src_ref=sums.at[sec], dst_ref=sums.at[0], send_sem=sem_zs.at[sec], recv_sem=sem_zr,
            device_id=(sec, t), device_id_type=MESH)

    @pl.when(first)
    def _():
        for other in range(tiles):
            @pl.when((other != t) | (j > 0))
            def _():
                copy_p(other).start()

            @pl.when((other == t) & (j == 0))
            def _():
                pieces[other] = of_tile(other)[...]

    @pl.when(first)
    def _():
        place_round(rounds - 1)

    @pl.when(jnp.logical_not(first))
    def _():
        send_patches()

        def placing(i, carry):
            place_round(i)
            return carry

        lax.fori_loop(0, rounds, placing, 0)

    @pl.when(s == 0)
    def _():
        def arrive(slot, carry):
            @pl.when(slot != t)
            def _():
                arrival_p(slot).wait_recv()

            return carry

        lax.fori_loop(0, heads * tiles, arrive, 0)
        total = pieces[0]
        for slot in range(1, heads * tiles):
            total = total + pieces[slot]
        for sec in range(sections):
            sums[sec] = jnp.broadcast_to(total[sec], sums.shape[1:])
        for sec in range(1, sections):
            copy_z(sec).start()
        for sec in range(1, sections):
            copy_z(sec).wait_send()

    @pl.when(s > 0)
    def _():
        copy_z(s).wait_recv()

    probe_out_ref[...] = sums[0]

    @pl.when(first)
    def _():
        for other in range(tiles):
            @pl.when((other != t) | (j > 0))
            def _():
                copy_p(other).wait_send()

    def sent(p, carry):
        @pl.when(p % size != j)
        def _():
            copy_w(p).wait_send()

        @pl.when(p % size == j)
        def _():
            for m in range(2):
                @pl.when(jnp.logical_not(last))
                def _():
                    copy_f(p, m).wait_send()

                @pl.when(jnp.logical_not(first) & ((j < size - 1) | (p < slots - 1)))
                def _():
                    copy_b(p, m).wait_send()

            def sent_piece(owner, inner):
                @pl.when(owner != j)
                def _():
                    copy_g(p, owner).wait_send()

                return inner

            lax.fori_loop(0, size, sent_piece, 0)

        return carry

    lax.fori_loop(0, slots, sent, 0)


GROUPS = {16: (2, 2, 4, 8), 8: (2, 2, 4), 4: (2, 2)}


def shards(sections, tiles, slab, probe, amplitudes, offsets, counts):
    layers, _, side, _ = slab.shape
    n = probe.shape[-1]
    slots = offsets.shape[0]
    sizes = GROUPS[sections]
    lines = 4 * n // sections
    share = lines // tiles
    piece = (sections, n) if share == 1 else (sections, share, n)
    sum_rows = max(8, share)
    hbm = pl.BlockSpec(memory_space=pl.ANY)
    vmem = pl.BlockSpec(memory_space=pltpu.VMEM)
    smem = pl.BlockSpec(memory_space=pltpu.SMEM)
    tab = jnp.asarray(tables(n))
    window = (layers, 2, n, n)
    wave = (slots, 2, 2, n, n)
    dma = pltpu.SemaphoreType.DMA
    grad, probe_grad = pl.pallas_call(
        functools.partial(kernel, sizes, tiles),
        out_shape=(
            jax.ShapeDtypeStruct(slab.shape, F32),
            jax.ShapeDtypeStruct((sum_rows, n), F32),
        ),
        in_specs=[hbm, hbm, hbm, smem, smem, hbm],
        out_specs=(vmem, vmem),
        scratch_shapes=[
            pltpu.VMEM(slab.shape, F32),
            pltpu.VMEM(probe.shape, F32),
            pltpu.VMEM(amplitudes.shape, BF16),
            pltpu.VMEM(tab.shape, BF16),
            pltpu.VMEM((side, side * layers * 4), BF16),
            pltpu.VMEM((slots,) + window, F32),
            pltpu.VMEM((slots,) + window, BF16),
            pltpu.VMEM((slots,) + window, BF16),
            pltpu.VMEM((slots * layers + 1, 2, 2, n, n), F32),
            pltpu.VMEM((2, 2, n, n), F32),
            pltpu.VMEM(window, BF16),
            pltpu.VMEM((slots,) + window, BF16),
            pltpu.VMEM((slots,) + window, BF16),
            pltpu.VMEM((sections, lines, n), F32),
            pltpu.VMEM(wave, BF16),
            pltpu.VMEM(wave, BF16),
            pltpu.VMEM(wave, BF16),
            pltpu.VMEM(wave, BF16),
            pltpu.VMEM((sizes[0] * tiles,) + piece, F32),
            pltpu.VMEM((sections, sum_rows, n), F32),
            dma((4,)),
            dma((slots,)), dma((slots,)),
            dma((slots,)), dma((slots,)),
            dma((slots, 2)), dma((slots, 2)),
            dma((slots, 2)), dma((slots, 2)),
            dma((tiles,)), dma((sizes[0] * tiles,)),
            dma((sections,)), dma,
            pltpu.SemaphoreType.REGULAR,
        ],
        compiler_params=pltpu.CompilerParams(
            collective_id=0, has_side_effects=True, vmem_limit_bytes=56 * 1024 * 1024),
    )(slab, probe, amplitudes, offsets, counts, tab)
    return grad, probe_grad[:share].reshape(-1)


def solution(mesh):
    body = functools.partial(shards, mesh.shape["sec"], mesh.shape["tile"])
    in_specs = (
        P("sec", None, "tile", None),
        P(),
        P("tile", None, None),
        P("tile", None),
        P("tile"),
    )
    out_specs = (P("sec", None, "tile", None), P(("sec", "tile")))
    return jax.shard_map(body, mesh=mesh, in_specs=in_specs, out_specs=out_specs, check_vma=False)
```

time: 221 us -> 157 us (0.71)
  Pallas kernels: 214 us -> 152 us
    pallas_call x1, Pallas kernels: 214 us -> 152 us  [shards(): pl.pallas_call(functools.partial(kernel, sizes, tiles), out_shape=(jax.Sh...]
    unnamed x12 -> x4, local copies, waits for them, and re-layouts: 5.41 us -> 2.97 us
where the time goes in v2:
time: 157 us
  Pallas kernels  152 us (97%)
  local copies, waits for them, and re-layouts  4.15 us (3%)
    pallas_call x1, Pallas kernels, shards(): pl.pallas_call(functools.partial(kernel, sizes, tiles), out_shape=(jax.Sh...  152 us

profile of v2, /device:TPU:1, one launch (start us, length us, event | category | flops | bytes accessed | tf_op | source)
XLA Modules:
  0.0 157.2 jit_solution(12426272976246124311)
XLA Ops:
  0.6 0.0 copy-start
  1.3 0.0 copy-done
  1.3 0.7 copy.8.offsets_ref
  2.0 151.8 %shard_map.77 = (f32[2,2,256,256]{3,2,1,0:T(8,128)}, f32[8,128]{1,0:T(8,128)}) custom-call(f32[2,2,256,256]{3,2,1,0:T(8,128)} %slab_hbm.1, f32[2,2,128,128]{3,2,1,0:T(8,128)} %probe_hbm.1, bf16[8,128,128]{2,1,0:T(8,128)(2,1)} %amps_hbm.1, s32[8,2]{1,0:T(8,128)} %copy.8.offsets_ref, s32[1]{0:T(128)S(6)} %copy.10.counts_ref, ...), custom_call_target="tpu_custom_call" | custom-call | tf_op jit(solution)/shard_map/pallas_call | solution.py:538
  153.8 1.2 slice_bitcast_fusion
  154.9 2.3 %copy.11 = f32[2,2,256,256]{3,2,1,0:T(8,128)} copy(f32[2,2,256,256]{3,2,1,0:T(8,128)} %get-tuple-element.8) | data formatting | bytes 2097152
Async XLA Ops:
  0.6 0.7 copy-start

commit v3 on v2

--- a/solution.py
+++ b/solution.py
@@ -76,8 +76,8 @@
     slab_hbm, probe_hbm, amps_hbm, offsets_ref, counts_ref, tab_hbm,
     grad_ref, probe_out_ref,
     slab_ref, probe_ref, amps_ref, tab_ref,
-    slab_parts, win, win_b, send_w, fields, cur, patch, send_g, recv_g, probe_acc,
-    send_f, recv_f, send_b, recv_b, pieces, sums,
+    slab_parts, win, win_b, send_w, fields, cur, patch, send_g, recv_g, probe_acc, stage,
+    send_f, recv_f, send_b, recv_b, pieces, sums, own_sum,
     sem_in, sem_sw, sem_rw, sem_sg, sem_rg, sem_sf, sem_rf, sem_sb, sem_rb, sem_ps, sem_pr, sem_zs, sem_zr, sem_go,
 ):
     n = probe_ref.shape[-1]
@@ -128,13 +128,17 @@
         def _():
             greet(start_after + (j + size * other) % size_after, t)
 
-    near_zero = first | ((start == starts[1]) & (j % heads == 0))
-
-    @pl.when(jnp.logical_not(near_zero))
+    per = sections // heads
+    strangers = [
+        int(k > 0 and not (k == 1 and (x - starts[1]) % heads == x // per)) for x, k in enumerate(group_of)]
+    from_strangers = [sum(strangers[x * per:(x + 1) * per]) if x < heads else 0 for x in range(sections)]
+    summer = s // per
+
+    @pl.when(by_section(s, strangers) == 1)
     def _():
-        greet(0, t)
-
-    @pl.when(s == 0)
+        greet(summer, t)
+
+    @pl.when(first)
     def _():
         def greet_tile(step, carry):
             for member in range(heads):
@@ -145,8 +149,7 @@
 
     greetings = size - 1
     greetings += jnp.where(first, 0, links_before) + jnp.where(last, 0, links_after)
-    greetings += jnp.where(first, tiles - 1, 0)
-    greetings += jnp.where(s == 0, sections - heads - max(1, sizes[1] // heads), 0)
+    greetings += jnp.where(first, (tiles - 1) * heads, 0) + by_section(s, from_strangers)
 
     grad_ref[...] = jnp.zeros_like(grad_ref)
     probe_acc[...] = jnp.zeros_like(probe_acc)
@@ -159,12 +162,12 @@
         shift = (at + len(planes)) * side
         slab_parts[:, shift:shift + side] = low
 
-    def cut(p, target):
+    def cut(p, target, parts):
         rows = one_hot(n, side, offsets_ref[p, 0], 0)
         columns = one_hot(side, n, 0, offsets_ref[p, 1])
         for at, (l, c) in enumerate(planes):
             value = None
-            for part in (at, at + len(planes)):
+            for part in range(at, at + parts * len(planes), len(planes)):
                 strip = dot(rows, slab_parts[:, part * side:(part + 1) * side]).astype(BF16)
                 term = dot(strip, columns)
                 value = term if value is None else value + term
@@ -210,12 +213,12 @@
 
             @pl.when(step < size)
             def _():
-                cut(p, send_w.at[p])
+                cut(p, send_w.at[p], 1)
                 copy_w(p).start()
 
             @pl.when(step == size)
             def _():
-                cut(p, win.at[i * size + j])
+                cut(p, win.at[i * size + j], 2)
 
             return carry
 
@@ -224,30 +227,33 @@
     pl.semaphore_wait(barrier, greetings)
     cut_round(0)
 
-    @pl.when(rounds > 1)
-    def _():
-        cut_round(1)
+    def cut_ahead(i, carry):
+        cut_round(i)
+        return carry
+
+    lax.fori_loop(1, jnp.where(first, jnp.minimum(rounds, 2), rounds), cut_ahead, 0)
 
     for copy in inputs[1:]:
         copy.wait()
 
-    def forward(i):
+    def forward(i, modes):
+        fresh = True if len(modes) == 2 else modes[0] == 0
         p = i * size + j
         base = i * size * 2
 
         @pl.when(first)
         def _():
-            for m in range(2):
+            for m in modes:
                 fields[base, m] = probe_ref[m]
 
         @pl.when(jnp.logical_not(first))
         def _():
-            for m in range(2):
+            for m in modes:
                 copy_f(p, m).wait_recv()
                 fields[base, m] = recv_f[p, m].astype(F32)
 
         def slices(owner, carry):
-            @pl.when(owner != j)
+            @pl.when((owner != j) & fresh)
             def _():
                 pair = i * size + owner
                 window_arrival(pair, owner).wait_recv()
@@ -257,11 +263,11 @@
                 at = base + 2 * owner + half
                 tr, ti = win[i * size + owner, half, 0], win[i * size + owner, half, 1]
                 results = []
-                for m in range(2):
+                for m in modes:
                     re, im = fields[at, m, 0], fields[at, m, 1]
                     results.append(two_sided(tab_ref, 0, 2, tr * re - ti * im, tr * im + ti * re))
-                for m in range(2):
-                    fields[at + 1, m, 0], fields[at + 1, m, 1] = results[m]
+                for m, result in zip(modes, results):
+                    fields[at + 1, m, 0], fields[at + 1, m, 1] = result
             return carry
 
         lax.fori_loop(0, size, slices, 0)
@@ -269,13 +275,14 @@
 
         @pl.when(jnp.logical_not(last))
         def _():
-            for m in range(2):
+            for m in modes:
                 send_f[p, m] = fields[end, m].astype(BF16)
                 copy_f(p, m).start()
 
-        @pl.when(last)
-        def _():
-            far(p, end)
+        if len(modes) == 2:
+            @pl.when(last)
+            def _():
+                far(p, end)
 
     def far(p, end):
         spectrum = [two_sided(tab_ref, 4, 6, fields[end, m, 0], fields[end, m, 1]) for m in range(2)]
@@ -286,13 +293,14 @@
         for m, (re, im) in enumerate(spectrum):
             cur[m, 0], cur[m, 1] = two_sided(tab_ref, 6, 4, factor * re, factor * im)
 
-    def backward(i):
+    def backward(i, modes):
+        whole = True if len(modes) == 2 else modes[0] == 1
         p = i * size + j
         base = i * size * 2
 
         @pl.when(jnp.logical_not(last))
         def _():
-            for m in range(2):
+            for m in modes:
                 copy_b(p, m).wait_recv()
                 cur[m] = recv_b[p, m].astype(F32)
 
@@ -301,22 +309,33 @@
             for half in (1, 0):
                 at = base + 2 * owner + half
                 tr, ti = win[i * size + owner, half, 0], win[i * size + owner, half, 1]
-                middle = [two_sided(tab_ref, 2, 0, cur[m, 0], cur[m, 1]) for m in range(2)]
+                middle = [two_sided(tab_ref, 2, 0, cur[m, 0], cur[m, 1]) for m in modes]
                 piece_re = piece_im = 0.0
-                for m, (re, im) in enumerate(middle):
+                for m, (re, im) in zip(modes, middle):
                     xr, xi = fields[at, m, 0], fields[at, m, 1]
                     piece_re += xr * re + xi * im
                     piece_im += xr * im - xi * re
                     cur[m, 0] = tr * re + ti * im
                     cur[m, 1] = tr * im - ti * re
-                patch[half, 0] = piece_re.astype(BF16)
-                patch[half, 1] = piece_im.astype(BF16)
-
-            @pl.when(owner == j)
+                piece = (piece_re, piece_im)
+                if len(modes) == 2:
+                    patch[half, 0], patch[half, 1] = [part.astype(BF16) for part in piece]
+                else:
+                    @pl.when(modes[0] == 0)
+                    def _():
+                        for c in range(2):
+                            fields[at, 0, c] = piece[c]
+
+                    @pl.when(modes[0] == 1)
+                    def _():
+                        for c in range(2):
+                            patch[half, c] = (fields[at, 0, c] + piece[c]).astype(BF16)
+
+            @pl.when((owner == j) & whole)
             def _():
                 recv_g[p] = patch[...]
 
-            @pl.when(owner != j)
+            @pl.when((owner != j) & whole)
             def _():
                 send_g[i * size + owner] = patch[...]
 
@@ -330,17 +349,15 @@
 
         @pl.when(jnp.logical_not(first))
         def _():
-            for m in range(2):
+            for m in modes:
                 send_b[p, m] = cur[m].astype(BF16)
                 copy_b(p, m).start()
 
         @pl.when(first)
         def _():
-            groups = sections // 4
-            for m in range(2):
+            for m in modes:
                 for c in range(2):
-                    where = pl.ds((2 * m + c) * groups, groups)
-                    probe_acc[where] += cur[m, c].reshape((groups,) + probe_acc.shape[1:])
+                    probe_acc[pl.ds(pl.multiple_of((2 * m + c) * n, n), n)] += cur[m, c]
 
     def send_patches():
         @pl.when(j == size - 1)
@@ -349,10 +366,11 @@
                 copy_b((rounds - 1) * size + j, m).wait_send()
 
             def allow(step, carry):
-                pl.semaphore_signal(sem_go, inc=1, device_id=(start + step, t), device_id_type=MESH)
+                pl.semaphore_signal(
+                    sem_go, inc=1, device_id=(start + (j + step) % size, t), device_id_type=MESH)
                 return carry
 
-            lax.fori_loop(0, size - 1, allow, 0)
+            lax.fori_loop(1, size, allow, 0)
 
         @pl.when(j < size - 1)
         def _():
@@ -383,80 +401,95 @@
 
         lax.fori_loop(0, size, one, 0)
 
+    alone = (size <= ALONE) & jnp.logical_not(last)
+
+    def by_modes(work, i):
+        @pl.when(alone)
+        def _():
+            def one(m, carry):
+                work(i, (m,))
+                return carry
+
+            lax.fori_loop(0, 2, one, 0)
+
+        @pl.when(jnp.logical_not(alone))
+        def _():
+            work(i, (0, 1))
+
     def turn(u, carry):
         onward = jnp.where(last, u % 2 == 0, u < rounds)
 
         @pl.when(onward)
         def _():
             i = jnp.where(last, u // 2, u)
-            forward(i)
-
-            @pl.when(i + 2 < rounds)
+            by_modes(forward, i)
+
+            @pl.when(first & (i + 2 < rounds))
             def _():
                 cut_round(i + 2)
 
         @pl.when(jnp.logical_not(onward))
         def _():
             i = jnp.where(last, u // 2, u - rounds)
-            backward(i)
-
-            @pl.when(first & (i > 0))
-            def _():
-                place_round(i - 1)
+            by_modes(backward, i)
 
         return carry
 
     lax.fori_loop(0, 2 * rounds, turn, 0)
 
-    share = probe_acc.shape[1] // tiles
-
-    def of_tile(other):
-        return probe_acc.at[:, other] if share == 1 else probe_acc.at[:, pl.ds(other * share, share)]
-
-    def copy_p(other):
-        return pltpu.make_async_remote_copy(
-            src_ref=of_tile(other), dst_ref=pieces.at[j * tiles + t], send_sem=sem_ps.at[other],
-            recv_sem=sem_pr.at[j * tiles + t], device_id=(0, other), device_id_type=MESH)
+    lines = 4 * n // sections
+    share = lines // tiles
+
+    def copy_p(member, other):
+        return pltpu.make_async_remote_copy(
+            src_ref=stage.at[other, :, pl.ds(member * per, per)], dst_ref=pieces.at[j * tiles + t],
+            send_sem=sem_ps.at[member * tiles + other], recv_sem=sem_pr.at[j * tiles + t],
+            device_id=(member, other), device_id_type=MESH)
 
     def arrival_p(slot):
         return pltpu.make_async_remote_copy(
-            src_ref=of_tile(0), dst_ref=pieces.at[slot], send_sem=sem_ps.at[0], recv_sem=sem_pr.at[slot],
-            device_id=(0, t), device_id_type=MESH)
-
-    def copy_z(sec):
-        return pltpu.make_async_remote_copy(
-            src_ref=sums.at[sec], dst_ref=sums.at[0], send_sem=sem_zs.at[sec], recv_sem=sem_zr,
-            device_id=(sec, t), device_id_type=MESH)
+            src_ref=stage.at[0, :, pl.ds(0, per)], dst_ref=pieces.at[slot], send_sem=sem_ps.at[0],
+            recv_sem=sem_pr.at[slot], device_id=(s, t), device_id_type=MESH)
+
+    def copy_z(at):
+        return pltpu.make_async_remote_copy(
+            src_ref=sums.at[at], dst_ref=own_sum, send_sem=sem_zs.at[at], recv_sem=sem_zr,
+            device_id=(j * per + at, t), device_id_type=MESH)
+
+    def each_piece(act):
+        def one(step, carry):
+            other = (t + step) % tiles
+            for member in range(heads):
+                @pl.when((step > 0) | (member != j))
+                def _():
+                    act(copy_p(member, other))
+
+            return carry
+
+        lax.fori_loop(0, tiles, one, 0)
 
     @pl.when(first)
     def _():
         for other in range(tiles):
-            @pl.when((other != t) | (j > 0))
-            def _():
-                copy_p(other).start()
-
-            @pl.when((other == t) & (j == 0))
-            def _():
-                pieces[other] = of_tile(other)[...]
-
-    @pl.when(first)
-    def _():
-        place_round(rounds - 1)
+            for k in range(share):
+                stage[other, k] = probe_acc[pl.ds(other * share + k, sections, stride=lines), :]
+        each_piece(lambda copy: copy.start())
+        pieces[j * tiles + t] = stage[t, :, pl.ds(j * per, per)]
 
     @pl.when(jnp.logical_not(first))
     def _():
         send_patches()
 
-        def placing(i, carry):
-            place_round(i)
-            return carry
-
-        lax.fori_loop(0, rounds, placing, 0)
-
-    @pl.when(s == 0)
+    def placing(i, carry):
+        place_round(i)
+        return carry
+
+    lax.fori_loop(0, rounds, placing, 0)
+
+    @pl.when(first)
     def _():
         def arrive(slot, carry):
-            @pl.when(slot != t)
+            @pl.when(slot != j * tiles + t)
             def _():
                 arrival_p(slot).wait_recv()
 
@@ -466,25 +499,32 @@
         total = pieces[0]
         for slot in range(1, heads * tiles):
             total = total + pieces[slot]
-        for sec in range(sections):
-            sums[sec] = jnp.broadcast_to(total[sec], sums.shape[1:])
-        for sec in range(1, sections):
-            copy_z(sec).start()
-        for sec in range(1, sections):
-            copy_z(sec).wait_send()
-
-    @pl.when(s > 0)
+        for at in range(per):
+            sums[at] = jnp.broadcast_to(total[:, at], sums.shape[1:])
+        for at in range(per):
+            @pl.when(j * per + at != s)
+            def _():
+                copy_z(at).start()
+
+            @pl.when(j * per + at == s)
+            def _():
+                own_sum[...] = sums[at]
+
+    @pl.when(summer != s)
     def _():
-        copy_z(s).wait_recv()
-
-    probe_out_ref[...] = sums[0]
+        pltpu.make_async_remote_copy(
+            src_ref=sums.at[0], dst_ref=own_sum, send_sem=sem_zs.at[0], recv_sem=sem_zr,
+            device_id=(summer, t), device_id_type=MESH).wait_recv()
+
+    probe_out_ref[...] = own_sum[0:share]
 
     @pl.when(first)
     def _():
-        for other in range(tiles):
-            @pl.when((other != t) | (j > 0))
-            def _():
-                copy_p(other).wait_send()
+        each_piece(lambda copy: copy.wait_send())
+        for at in range(per):
+            @pl.when(j * per + at != s)
+            def _():
+                copy_z(at).wait_send()
 
     def sent(p, carry):
         @pl.when(p % size != j)
@@ -516,6 +556,7 @@
     lax.fori_loop(0, slots, sent, 0)
 
 
+ALONE = 2
 GROUPS = {16: (2, 2, 4, 8), 8: (2, 2, 4), 4: (2, 2)}
 
 
@@ -526,9 +567,9 @@
     sizes = GROUPS[sections]
     lines = 4 * n // sections
     share = lines // tiles
-    piece = (sections, n) if share == 1 else (sections, share, n)
+    per = sections // sizes[0]
     sum_rows = max(8, share)
-    hbm = pl.BlockSpec(memory_space=pl.ANY)
+    hbm = pl.BlockSpec(memory_space=pltpu.HBM)
     vmem = pl.BlockSpec(memory_space=pltpu.VMEM)
     smem = pl.BlockSpec(memory_space=pltpu.SMEM)
     tab = jnp.asarray(tables(n))
@@ -539,7 +580,7 @@
         functools.partial(kernel, sizes, tiles),
         out_shape=(
             jax.ShapeDtypeStruct(slab.shape, F32),
-            jax.ShapeDtypeStruct((sum_rows, n), F32),
+            jax.ShapeDtypeStruct((share, n), F32),
         ),
         in_specs=[hbm, hbm, hbm, smem, smem, hbm],
         out_specs=(vmem, vmem),
@@ -557,26 +598,28 @@
             pltpu.VMEM(window, BF16),
             pltpu.VMEM((slots,) + window, BF16),
             pltpu.VMEM((slots,) + window, BF16),
-            pltpu.VMEM((sections, lines, n), F32),
+            pltpu.VMEM((4 * n, n), F32),
+            pltpu.VMEM((tiles, share, sections, n), F32),
             pltpu.VMEM(wave, BF16),
             pltpu.VMEM(wave, BF16),
             pltpu.VMEM(wave, BF16),
             pltpu.VMEM(wave, BF16),
-            pltpu.VMEM((sizes[0] * tiles,) + piece, F32),
-            pltpu.VMEM((sections, sum_rows, n), F32),
+            pltpu.VMEM((sizes[0] * tiles, share, per, n), F32),
+            pltpu.VMEM((per, sum_rows, n), F32),
+            pltpu.VMEM((sum_rows, n), F32),
             dma((4,)),
             dma((slots,)), dma((slots,)),
             dma((slots,)), dma((slots,)),
             dma((slots, 2)), dma((slots, 2)),
             dma((slots, 2)), dma((slots, 2)),
-            dma((tiles,)), dma((sizes[0] * tiles,)),
-            dma((sections,)), dma,
+            dma((sizes[0] * tiles,)), dma((sizes[0] * tiles,)),
+            dma((per,)), dma,
             pltpu.SemaphoreType.REGULAR,
         ],
         compiler_params=pltpu.CompilerParams(
             collective_id=0, has_side_effects=True, vmem_limit_bytes=56 * 1024 * 1024),
     )(slab, probe, amplitudes, offsets, counts, tab)
-    return grad, probe_grad[:share].reshape(-1)
+    return grad, probe_grad.reshape(-1)
 
 
 def solution(mesh):

time: 157 us -> 149 us (0.949)
  Pallas kernels: 152 us -> 144 us
    pallas_call x1, Pallas kernels: 152 us -> 144 us  [shards(): pl.pallas_call(functools.partial(kernel, sizes, tiles), out_shape=(jax.Sh...]
    unnamed x4 -> x7, local copies, waits for them, and re-layouts: 2.97 us -> 3.49 us
where the time goes in v3:
time: 149 us
  Pallas kernels  144 us (97%)
  local copies, waits for them, and re-layouts  3.49 us (2%)
    pallas_call x1, Pallas kernels, shards(): pl.pallas_call(functools.partial(kernel, sizes, tiles), out_shape=(jax.Sh...  144 us
    unnamed x7, local copies, waits for them, and re-layouts  3.49 us

profile of v3, /device:TPU:1, one launch (start us, length us, event | category | flops | bytes accessed | tf_op | source)
XLA Modules:
  0.0 149.0 jit_solution(7397500181277073427)
XLA Ops:
  0.6 0.0 copy-start
  1.3 0.0 copy-done
  1.3 0.7 copy.8.offsets_ref
  2.0 144.2 %shard_map.77 = (f32[2,2,256,256]{3,2,1,0:T(8,128)}, f32[1,128]{1,0:T(1,128)}) custom-call(f32[2,2,256,256]{3,2,1,0:T(8,128)} %slab_hbm.1, f32[2,2,128,128]{3,2,1,0:T(8,128)} %probe_hbm.1, bf16[8,128,128]{2,1,0:T(8,128)(2,1)} %amps_hbm.1, s32[8,2]{1,0:T(8,128)} %copy.8.offsets_ref, s32[1]{0:T(128)S(6)} %copy.11.counts_ref, ...), custom_call_target="tpu_custom_call" | custom-call | tf_op jit(solution)/shard_map/pallas_call | solution.py:579
  146.2 0.0 copy-start.1
  146.2 2.3 %copy.12 = f32[2,2,256,256]{3,2,1,0:T(8,128)} copy(f32[2,2,256,256]{3,2,1,0:T(8,128)} %get-tuple-element.8) | data formatting | bytes 2097152
  148.5 0.0 copy-done.1
  148.5 0.5 copy.13
Async XLA Ops:
  0.6 0.7 copy-start
  146.2 2.3 %copy-start.1 = (f32[1,128]{1,0:T(1,128)S(1)}, f32[1,128]{1,0:T(1,128)}, u32[]{:S(2)}) copy-start(f32[1,128]{1,0:T(1,128)} %get-tuple-element.5) | copy-start | bytes 1540

commit v4 on v3

--- a/solution.py
+++ b/solution.py
@@ -231,7 +231,7 @@
         cut_round(i)
         return carry
 
-    lax.fori_loop(1, jnp.where(first, jnp.minimum(rounds, 2), rounds), cut_ahead, 0)
+    lax.fori_loop(1, jnp.where(first, 1, rounds), cut_ahead, 0)
 
     for copy in inputs[1:]:
         copy.wait()
@@ -424,9 +424,9 @@
             i = jnp.where(last, u // 2, u)
             by_modes(forward, i)
 
-            @pl.when(first & (i + 2 < rounds))
-            def _():
-                cut_round(i + 2)
+            @pl.when(first & (i + 1 < rounds))
+            def _():
+                cut_round(i + 1)
 
         @pl.when(jnp.logical_not(onward))
         def _():

time: 149 us -> 148 us (level)
  Pallas kernels: 144 us -> 142 us
    pallas_call x1, Pallas kernels: 144 us -> 142 us  [shards(): pl.pallas_call(functools.partial(kernel, sizes, tiles), out_shape=(jax.Sh...]
where the time goes in v4:
time: 148 us; the launch traced here: 147 us
  Pallas kernels  142 us (96%)
  local copies, waits for them, and re-layouts  3.49 us (2%)
    pallas_call x1, Pallas kernels, shards(): pl.pallas_call(functools.partial(kernel, sizes, tiles), out_shape=(jax.Sh...  142 us
    unnamed x7, local copies, waits for them, and re-layouts  3.49 us

profile of v4, /device:TPU:1, one launch (start us, length us, event | category | flops | bytes accessed | tf_op | source)
XLA Modules:
  0.0 147.1 jit_solution(11110164012659708893)
XLA Ops:
  0.6 0.0 copy-start
  1.3 0.0 copy-done
  1.3 0.7 copy.8.offsets_ref
  2.0 142.3 %shard_map.77 = (f32[2,2,256,256]{3,2,1,0:T(8,128)}, f32[1,128]{1,0:T(1,128)}) custom-call(f32[2,2,256,256]{3,2,1,0:T(8,128)} %slab_hbm.1, f32[2,2,128,128]{3,2,1,0:T(8,128)} %probe_hbm.1, bf16[8,128,128]{2,1,0:T(8,128)(2,1)} %amps_hbm.1, s32[8,2]{1,0:T(8,128)} %copy.8.offsets_ref, s32[1]{0:T(128)S(6)} %copy.11.counts_ref, ...), custom_call_target="tpu_custom_call" | custom-call | tf_op jit(solution)/shard_map/pallas_call | solution.py:579
  144.3 0.0 copy-start.1
  144.3 2.3 %copy.12 = f32[2,2,256,256]{3,2,1,0:T(8,128)} copy(f32[2,2,256,256]{3,2,1,0:T(8,128)} %get-tuple-element.8) | data formatting | bytes 2097152
  146.6 0.0 copy-done.1
  146.6 0.5 copy.13
Async XLA Ops:
  0.6 0.7 copy-start
  144.3 2.3 %copy-start.1 = (f32[1,128]{1,0:T(1,128)S(1)}, f32[1,128]{1,0:T(1,128)}, u32[]{:S(2)}) copy-start(f32[1,128]{1,0:T(1,128)} %get-tuple-element.5) | copy-start | bytes 1540

commit v5 on v4

--- a/solution.py
+++ b/solution.py
@@ -557,7 +557,7 @@
 
 
 ALONE = 2
-GROUPS = {16: (2, 2, 4, 8), 8: (2, 2, 4), 4: (2, 2)}
+GROUPS = {16: (1, 1, 2, 4, 8), 8: (2, 2, 4), 4: (2, 2)}
 
 
 def shards(sections, tiles, slab, probe, amplitudes, offsets, counts):

time: 148 us -> 153 us (1.034)
  Pallas kernels: 142 us -> 148 us
    pallas_call x1, Pallas kernels: 142 us -> 148 us  [shards(): pl.pallas_call(functools.partial(kernel, sizes, tiles), out_shape=(jax.Sh...]
where the time goes in v5:
time: 153 us; the launch traced here: 152 us
  Pallas kernels  148 us (97%)
  local copies, waits for them, and re-layouts  3.49 us (2%)
    pallas_call x1, Pallas kernels, shards(): pl.pallas_call(functools.partial(kernel, sizes, tiles), out_shape=(jax.Sh...  148 us
    unnamed x7, local copies, waits for them, and re-layouts  3.49 us

profile of v5, /device:TPU:1, one launch (start us, length us, event | category | flops | bytes accessed | tf_op | source)
XLA Modules:
  0.0 152.5 jit_solution(10836840025294448972)
XLA Ops:
  0.6 0.0 copy-start
  1.3 0.0 copy-done
  1.3 0.7 copy.8.offsets_ref
  2.0 147.7 %shard_map.77 = (f32[2,2,256,256]{3,2,1,0:T(8,128)}, f32[1,128]{1,0:T(1,128)}) custom-call(f32[2,2,256,256]{3,2,1,0:T(8,128)} %slab_hbm.1, f32[2,2,128,128]{3,2,1,0:T(8,128)} %probe_hbm.1, bf16[8,128,128]{2,1,0:T(8,128)(2,1)} %amps_hbm.1, s32[8,2]{1,0:T(8,128)} %copy.8.offsets_ref, s32[1]{0:T(128)S(6)} %copy.11.counts_ref, ...), custom_call_target="tpu_custom_call" | custom-call | tf_op jit(solution)/shard_map/pallas_call | solution.py:579
  149.7 0.0 copy-start.1
  149.7 2.3 %copy.12 = f32[2,2,256,256]{3,2,1,0:T(8,128)} copy(f32[2,2,256,256]{3,2,1,0:T(8,128)} %get-tuple-element.8) | data formatting | bytes 2097152
  152.0 0.0 copy-done.1
  152.0 0.5 copy.13
Async XLA Ops:
  0.6 0.7 copy-start
  149.7 2.3 %copy-start.1 = (f32[1,128]{1,0:T(1,128)S(1)}, f32[1,128]{1,0:T(1,128)}, u32[]{:S(2)}) copy-start(f32[1,128]{1,0:T(1,128)} %get-tuple-element.5) | copy-start | bytes 1540
